TPU v7x, 128 devices: a whole 4x4x4 slice. The times are simulated.
128 devices in a mesh: gx: 32 (over x, y, core), gy: 4 (over z).
Axes of the slice: x: 4, y: 4, z: 4, core: 2. Of those that a mesh axis runs over, the one named last changes fastest.
Arguments:
- right_side: float32 [1024, 512, 128], P('gx', 'gy'), may hold values from -8 to 8
- sea_mask: int32 [1024, 512], P('gx', 'gy'), may hold values 0 or 1
- vertical_coupling: float32 [127], replicated, may hold values from 1 to 16
Outputs:
- solution_field: float32 [1024, 512, 128], P('gx', 'gy')
- residual: float32 [1024, 512, 128], P('gx', 'gy')
All inputs are finite; a program needn't handle non-finite values. No bound on the sum of `sea_mask` on one device may be relied on, other than what follows from the above.
Results may differ from a plain program's by a relative error of at most 0.0003.
Values sent between devices are 32-bit elements; how exact they have to be, the bound alone decides.
A program may use at most 128 MiB of HBM per device.

v0:
```python
import jax
import jax.numpy as jnp
from jax import lax
from jax.sharding import PartitionSpec as P

ITERS = 3
SWEEPS = 4


shift_term = 0.1
coarse_diag = 4.4
damping = 0.8


def padded_2(cells, sides, width):
    for axis, dim in sides:
        count = lax.axis_size(axis)
        ends = count - 1
        head = lax.slice_in_dim(cells, 0, width, axis=dim)
        tail = lax.slice_in_dim(cells, cells.shape[dim] - width, cells.shape[dim], axis=dim)
        cells = jnp.concatenate(
            [
                lax.ppermute(tail, axis, [(i, (i + 1) % count) for i in range(ends)]),
                cells,
                lax.ppermute(head, axis, [((i + 1) % count, i) for i in range(ends)]),
            ],
            axis=dim,
        )
    return cells


def line_inverse(coupling, diag_value, factor):
    count = coupling.shape[0] + 1
    upper = jnp.pad(coupling, (0, 1))
    lower = jnp.pad(coupling, (1, 0))
    matrix = factor * (jnp.diag(upper + lower) - jnp.diag(coupling, 1) - jnp.diag(coupling, -1))
    matrix = matrix + diag_value * jnp.eye(count, dtype=matrix.dtype)
    chol = jnp.linalg.cholesky(matrix)
    return jax.scipy.linalg.cho_solve((chol, True), jnp.eye(count, dtype=matrix.dtype))


def line_apply(field, inverse):
    shape = field.shape
    flat = jnp.dot(field.reshape(-1, shape[-1]), inverse, precision=lax.Precision.HIGHEST)
    return flat.reshape(shape)


def line_smooth(field, maskf, inverse):
    return maskf[..., None] * line_apply(field, inverse) + (1.0 - maskf[..., None]) * field


def operate_padded(padded, mask_pad, coupling):
    value = padded[1:-1, 1:-1]
    maskf = mask_pad[1:-1, 1:-1]
    horiz = mask_pad[2:, 1:-1, None] * (value - padded[2:, 1:-1])
    horiz = horiz + mask_pad[:-2, 1:-1, None] * (value - padded[:-2, 1:-1])
    horiz = horiz + mask_pad[1:-1, 2:, None] * (value - padded[1:-1, 2:])
    horiz = horiz + mask_pad[1:-1, :-2, None] * (value - padded[1:-1, :-2])
    flux = coupling * (value[..., :-1] - value[..., 1:])
    vertical = jnp.pad(flux, ((0, 0), (0, 0), (0, 1))) - jnp.pad(flux, ((0, 0), (0, 0), (1, 0)))
    inner = shift_term * value + vertical + horiz
    return maskf[..., None] * inner + (1.0 - maskf[..., None]) * value


def coarse_sweep(padded, target):
    value = padded[1:-1, 1:-1]
    beside = padded[2:, 1:-1] + padded[:-2, 1:-1] + padded[1:-1, 2:] + padded[1:-1, :-2]
    applied = coarse_diag * value - beside
    return value + damping * (target - applied) / coarse_diag


def shards(right_side, sea_mask, vertical_coupling):
    maskf = sea_mask.astype(jnp.float32)
    mask_pad = padded_2(maskf, (("gx", 0), ("gy", 1)), 1)
    inv_fine = line_inverse(vertical_coupling, 4.1, 1.0)
    inv_coarse = line_inverse(vertical_coupling, 4.4, 4.0)

    def operate(field):
        padded = padded_2(field, (("gx", 0), ("gy", 1)), 1)
        return operate_padded(padded, mask_pad, vertical_coupling)

    def coarse_solve(target):
        level = jnp.zeros_like(target)
        for sweep in range(SWEEPS):
            padded = padded_2(level, (("gx", 0), ("gy", 1)), 1)
            level = coarse_sweep(padded, target)
        return level

    def precondition(source):
        first = line_smooth(source, maskf, inv_fine)
        first_pad = padded_2(first, (("gx", 0), ("gy", 1)), 1)
        left = source - operate_padded(first_pad, mask_pad, vertical_coupling)
        nx, ny, nz = left.shape
        coarse = left.reshape(nx // 2, 2, ny // 2, 2, nz).sum(axis=(1, 3))
        corr = line_apply(coarse, inv_coarse)
        target = jnp.sum(coarse, axis=2) / nz
        level = coarse_solve(target)
        corr = corr + level[..., None]
        fine = jnp.repeat(jnp.repeat(corr, 2, axis=0), 2, axis=1)
        guess = first + maskf[..., None] * fine
        guess_pad = padded_2(guess, (("gx", 0), ("gy", 1)), 1)
        remain = source - operate_padded(guess_pad, mask_pad, vertical_coupling)
        return guess + line_smooth(remain, maskf, inv_fine)

    solution_field = jnp.zeros_like(right_side)
    residual = right_side
    u_vec = precondition(residual)
    w_vec = operate(u_vec)
    z_vec = q_vec = s_vec = p_vec = jnp.zeros_like(right_side)
    gamma_prev = jnp.float32(1.0)
    alpha_prev = jnp.float32(1.0)
    for step in range(ITERS):
        gamma, delta = lax.psum((jnp.sum(residual * u_vec), jnp.sum(w_vec * u_vec)), ("gx", "gy"))
        m_vec = precondition(w_vec)
        n_vec = operate(m_vec)
        if step == 0:
            beta = jnp.zeros_like(gamma)
            alpha = gamma / delta
        else:
            beta = gamma / gamma_prev
            alpha = gamma / (delta - beta * gamma / alpha_prev)
        z_vec = n_vec + beta * z_vec
        q_vec = m_vec + beta * q_vec
        s_vec = w_vec + beta * s_vec
        p_vec = u_vec + beta * p_vec
        solution_field = solution_field + alpha * p_vec
        residual = residual - alpha * s_vec
        u_vec = u_vec - alpha * q_vec
        w_vec = w_vec - alpha * z_vec
        gamma_prev = gamma
        alpha_prev = alpha
    return (solution_field, residual)


def solution(mesh):
    placed = (P("gx", "gy", None), P("gx", "gy"), P())
    return jax.shard_map(
        shards,
        mesh=mesh,
        in_specs=placed,
        out_specs=(P("gx", "gy", None), P("gx", "gy", None)),
        check_vma=False,
    )
```

profile of v0, /device:TPU:0, one launch (start us, length us, event | category | flops | bytes accessed | tf_op | source)
XLA Modules:
  0.0 703.5 jit_solution(9188494703184163690)
XLA Ops:
  4.0 4.9 collective-permute-start.2
  12.0 11.7 %cholesky.44 = f32[128,128]{1,0:T(8,128)S(1)} custom-call(f32[128,128]{1,0:T(8,128)S(1)} %get-tuple-element.112), custom_call_target="Cholesky" | custom-call | tf_op jit(solution)/shard_map/jit(cholesky)/cholesky | solution.py:38
  25.1 9.8 %custom-call.8 = f32[1,128,128]{1,2,0:T(8,128)S(1)} custom-call(f32[1,128,128]{2,1,0:T(8,128)S(1)} %fusion.172), custom_call_target="InvertDiagBlocksLowerTriangular" | custom-call | tf_op jit(solution)/shard_map/jit(_cho_solve)/triangular_solve | solution.py:39
  35.4 3.5 convolution_bitcast_fusion
  40.7 3.6 multiply_add_fusion.7
  44.3 4.5 collective-permute-start.3
  50.8 11.7 %cholesky.55 = f32[128,128]{1,0:T(8,128)S(1)} custom-call(f32[128,128]{1,0:T(8,128)S(1)} %get-tuple-element.111), custom_call_target="Cholesky" | custom-call | tf_op jit(solution)/shard_map/jit(cholesky)/cholesky | solution.py:38
  66.5 5.1 collective-permute-start.11
  73.1 4.5 collective-permute-start.6
  79.0 4.5 collective-permute-start.7
  85.0 7.4 %fusion.272 = (f32[32,128]{1,0:T(8,128)S(1)}, f32[32,128,128]{2,1,0:T(8,128)}) fusion(f32[32,128,128]{2,1,0:T(8,128)S(1)} %copy-done.12, f32[32,128,128]{2,1,0:T(8,128)S(1)} %multiply_add_fusion.7, f32[32,128]{1,0:T(8,128)S(1)} %broadcast_subtract_fusion, f32[1,128,128]{2,1,0:T(8,128)S(1)} %collective-permute-done.1, ...), kind=kLoop, calls=%fused_computation.522 | loop fusion | flops 14675968 | bytes 8652800 | tf_op jit(solution)/shard_map/reduce_sum | solution.py:96
  98.6 9.8 %custom-call.9 = f32[1,128,128]{1,2,0:T(8,128)S(1)} custom-call(f32[1,128,128]{2,1,0:T(8,128)S(1)} %fusion.173), custom_call_target="InvertDiagBlocksLowerTriangular" | custom-call | tf_op jit(solution)/shard_map/jit(_cho_solve)/triangular_solve | solution.py:39
  109.8 4.7 collective-permute-start.15
  115.9 5.7 collective-permute-start.17
  123.2 3.5 collective-permute-done.16
  128.1 4.8 collective-permute-start.19
  134.4 3.4 collective-permute-start.21
  139.3 3.2 reduce_sum.129
  143.9 5.0 collective-permute-start.23
  156.3 3.9 collective-permute-done.24
  161.6 5.0 collective-permute-start.27
  168.0 8.7 %add_add_fusion.2 = f32[32,128,128]{2,1,0:T(8,128)S(1)} fusion(f32[32,128,128]{2,1,0:T(8,128)S(1)} %multiply_add_fusion.6, f32[32,128,128]{2,1,0:T(8,128)S(1)} %copy-done.13, f32[1,128,128]{2,1,0:T(8,128)S(1)} %collective-permute-done.24, f32[1,128,128]{2,1,0:T(8,128)S(1)} %collective-permute-done.25, f32[34,1,128]{2,1,0:T(1,128)S(1)} %collective-permute-done.27, ...), kind=kOutput, calls=%fused_computation.246 | convolution fusion | flops 835715072 | bytes 8701952 | tf_op jit(solution)/shard_map/dot_general | solution.py:44
  176.7 4.0 collective-permute-start.29
  182.0 5.0 collective-permute-done.28
  188.4 4.8 collective-permute-start.31
  194.7 6.1 multiply_reduce_fusion.4
  203.0 5.1 collective-permute-start.33
  209.4 4.3 collective-permute-done.32
  215.1 5.0 collective-permute-start.35
  221.4 6.4 fusion.268
  229.0 4.1 collective-permute-start.37
  234.5 4.1 collective-permute-done.36
  239.9 4.8 collective-permute-start.39
  246.2 5.7 collective-permute-start.41
  257.2 4.8 collective-permute-start.43
  263.5 4.9 collective-permute-start.45
  269.7 3.2 reduce_sum.135
  274.3 4.7 collective-permute-start.47
  283.4 4.4 collective-permute-start.49
  289.2 4.2 collective-permute-done.48
  294.7 5.0 collective-permute-start.51
  301.1 8.7 %add_add_fusion.1 = f32[32,128,128]{2,1,0:T(8,128)S(1)} fusion(f32[32,128,128]{2,1,0:T(8,128)S(1)} %multiply_add_fusion.4, f32[32,128,128]{2,1,0:T(8,128)S(1)} %copy-done.9, f32[1,128,128]{2,1,0:T(8,128)S(1)} %collective-permute-done.48, f32[1,128,128]{2,1,0:T(8,128)S(1)} %collective-permute-done.49, f32[34,1,128]{2,1,0:T(1,128)S(1)} %collective-permute-done.51, ...), kind=kOutput, calls=%fused_computation.240 | convolution fusion | flops 835715072 | bytes 8701952 | tf_op jit(solution)/shard_map/dot_general | solution.py:44
  311.2 4.0 collective-permute-start.53
  316.8 83.7 %all-reduce.24 = (f32[]{:T(128)}, f32[]{:T(128)}) all-reduce(f32[]{:T(128)} %get-tuple-element.9, f32[]{:T(128)} %get-tuple-element.8), channel_id=1, replica_groups=mesh['gx'=32,'gy'=4] {'gx','gy'}, use_global_device_ids=true, to_apply=%region_6.9 | all-reduce | flops 2 | bytes 16 | tf_op jit(solution)/shard_map/psum | solution.py:113
  404.3 4.8 collective-permute-start.55
  410.5 7.4 %multiply_reduce_fusion.2 = (f32[]{:T(128)}, f32[]{:T(128)}, f32[32,128,128]{2,1,0:T(8,128)}, f32[32,128,128]{2,1,0:T(8,128)S(1)}) fusion(f32[32,128,128]{2,1,0:T(8,128)S(1)} %add_add_fusion.2, f32[32,128,128]{2,1,0:T(8,128)S(1)} %copy-done.5, f32[]{:T(128)S(6)} %div.80, f32[32,128,128]{2,1,0:T(8,128)S(1)} %copy-done.14, f32[32,128,128]{2,1,0:T(8,128)S(1)} %copy-done.10, ...), kind=kLoop, calls=%fused_computation.236 | loop fusion | flops 18874368 | bytes 14927884 | tf_op jit(solution)/shard_map/reduce_sum | solution.py:113
  425.9 4.8 collective-permute-start.59
  432.2 7.0 fusion.266
  441.1 3.1 collective-permute-start.61
  448.9 4.8 collective-permute-start.63
  455.2 3.4 collective-permute-start.65
  463.6 4.8 collective-permute-start.67
  469.9 3.4 collective-permute-start.69
  474.6 3.2 reduce_sum.141
  479.2 4.5 collective-permute-start.71
  492.3 3.9 collective-permute-done.72
  497.6 5.2 collective-permute-start.75
  504.0 8.8 %add_add_fusion = f32[32,128,128]{2,1,0:T(8,128)S(1)} fusion(f32[32,128,128]{2,1,0:T(8,128)S(1)} %multiply_add_fusion.1, f32[32,128,128]{2,1,0:T(8,128)S(1)} %copy-done.16, f32[1,128,128]{2,1,0:T(8,128)S(1)} %collective-permute-done.72, f32[1,128,128]{2,1,0:T(8,128)S(1)} %collective-permute-done.73, f32[34,1,128]{2,1,0:T(1,128)S(1)} %collective-permute-done.75, ...), kind=kOutput, calls=%fused_computation.231 | convolution fusion | flops 835715072 | bytes 8701952 | tf_op jit(solution)/shard_map/dot_general | solution.py:44
  514.2 4.1 collective-permute-start.77
  519.6 80.7 %all-reduce.23 = (f32[]{:T(128)}, f32[]{:T(128)}) all-reduce(f32[]{:T(128)} %get-tuple-element.5, f32[]{:T(128)} %get-tuple-element.4), channel_id=1, replica_groups=mesh['gx'=32,'gy'=4] {'gx','gy'}, use_global_device_ids=true, to_apply=%region_13.16 | all-reduce | flops 2 | bytes 16 | tf_op jit(solution)/shard_map/psum | solution.py:113
  607.5 4.8 collective-permute-start.79
  613.7 13.4 %multiply_reduce_fusion = (f32[]{:T(128)}, f32[]{:T(128)}, f32[32,128,128]{2,1,0:T(8,128)}, f32[32,128,128]{2,1,0:T(8,128)}) fusion(f32[32,128,128]{2,1,0:T(8,128)} %get-tuple-element.18, f32[32,128,128]{2,1,0:T(8,128)S(1)} %copy-done.17, f32[32,128,128]{2,1,0:T(8,128)S(1)} %copy-done.11, f32[]{:T(128)S(6)} %div.86, f32[]{:T(128)S(6)} %div.88, ...), kind=kLoop, calls=%fused_computation.228 | loop fusion | flops 36700160 | bytes 21368852 | tf_op jit(solution)/shard_map/reduce_sum | solution.py:113
  627.2 63.8 %all-reduce.22 = (f32[]{:T(128)}, f32[]{:T(128)}) all-reduce(f32[]{:T(128)} %get-tuple-element.7, f32[]{:T(128)} %get-tuple-element.6), channel_id=1, replica_groups=mesh['gx'=32,'gy'=4] {'gx','gy'}, use_global_device_ids=true, to_apply=%region_20.23 | all-reduce | flops 2 | bytes 16 | tf_op jit(solution)/shard_map/psum | solution.py:113
  694.9 6.0 multiply_subtract_fusion
  (282 shorter events, 132.5 us)
Async XLA Ops:
  0.6 62.6 %collective-permute-start.9 = (f32[1,64]{1,0:T(1,128)S(1)}, f32[1,64]{1,0:T(1,128)S(1)}, u32[]{:S(2)}, u32[]{:S(2)}) collective-permute-start(f32[1,64]{1,0:T(1,128)S(1)} %broadcast.165), channel_id=1, source_target_pairs={{0,4},{4,8},{8,12},{12,16},{16,20},{20,24},{24,28},{28,32},{32,36}... | collective-permute-start | bytes 776 | tf_op jit(solution)/shard_map/ppermute | solution.py:23
  1.9 62.6 %collective-permute-start.8 = (f32[1,64]{1,0:T(1,128)S(1)}, f32[1,64]{1,0:T(1,128)S(1)}, u32[]{:S(2)}, u32[]{:S(2)}) collective-permute-start(f32[1,64]{1,0:T(1,128)S(1)} %broadcast.165), channel_id=1, source_target_pairs={{4,0},{8,4},{12,8},{16,12},{20,16},{24,20},{28,24},{32,28},{36,32}... | collective-permute-start | bytes 776 | tf_op jit(solution)/shard_map/ppermute | solution.py:25
  4.0 62.5 %collective-permute-start.2 = (f32[1,128]{1,0:T(1,128)S(1)}, f32[1,128]{1,0:T(1,128)S(1)}, u32[]{:S(2)}, u32[]{:S(2)}) collective-permute-start(f32[1,128]{1,0:T(1,128)S(1)} %get-tuple-element.71), channel_id=1, source_target_pairs={{0,4},{4,8},{8,12},{12,16},{16,20},{20,24},{24,28},{28,32},{32,36}... | collective-permute-start | bytes 1544 | tf_op jit(solution)/shard_map/ppermute | solution.py:23
  8.9 62.8 %collective-permute-start = (f32[1,128]{1,0:T(1,128)S(1)}, f32[1,128]{1,0:T(1,128)S(1)}, u32[]{:S(2)}, u32[]{:S(2)}) collective-permute-start(f32[1,128]{1,0:T(1,128)S(1)} %get-tuple-element.72), channel_id=1, source_target_pairs={{4,0},{8,4},{12,8},{16,12},{20,16},{24,20},{28,24},{32,28},{36,32}... | collective-permute-start | bytes 1544 | tf_op jit(solution)/shard_map/ppermute | solution.py:25
  44.3 28.7 %collective-permute-start.3 = (f32[1,128,128]{2,1,0:T(8,128)S(1)}, f32[1,128,128]{2,1,0:T(8,128)S(1)}, u32[]{:S(2)}, u32[]{:S(2)}) collective-permute-start(f32[1,128,128]{2,1,0:T(8,128)S(1)} %get-tuple-element.63), channel_id=1, source_target_pairs={{0,4},{4,8},{8,12},{12,16},{16,20},{20,24},{24,28},{28,32},{32,36}... | collective-permute-start | bytes 196616 | tf_op jit(solution)/shard_map/ppermute | solution.py:23
  63.2 14.4 %collective-permute-start.1 = (f32[1,128,128]{2,1,0:T(8,128)S(1)}, f32[1,128,128]{2,1,0:T(8,128)S(1)}, u32[]{:S(2)}, u32[]{:S(2)}) collective-permute-start(f32[1,128,128]{2,1,0:T(8,128)S(1)} %get-tuple-element.64), channel_id=1, source_target_pairs={{4,0},{8,4},{12,8},{16,12},{20,16},{24,20},{28,24},{32,28},{36,32}... | collective-permute-start | bytes 196616 | tf_op jit(solution)/shard_map/ppermute | solution.py:25
  65.2 28.4 %collective-permute-start.10 = (f32[18,1]{1,0:T(8,128)}, f32[18,1]{1,0:T(8,128)S(1)}, u32[]{:S(2)}, u32[]{:S(2)}) collective-permute-start(f32[18,1]{1,0:T(8,128)} %get-tuple-element.91), channel_id=1, source_target_pairs={{1,0},{2,1},{3,2},{5,4},{6,5},{7,6},{9,8},{10,9},{11,10},{13,12},{... | collective-permute-start | bytes 224 | tf_op jit(solution)/shard_map/ppermute | solution.py:25
  66.5 27.1 %collective-permute-start.11 = (f32[18,1]{1,0:T(8,128)}, f32[18,1]{1,0:T(8,128)}, u32[]{:S(2)}, u32[]{:S(2)}) collective-permute-start(f32[18,1]{1,0:T(8,128)} %get-tuple-element.92), channel_id=1, source_target_pairs={{0,1},{1,2},{2,3},{4,5},{5,6},{6,7},{8,9},{9,10},{10,11},{12,13},{... | collective-permute-start | bytes 224 | tf_op jit(solution)/shard_map/ppermute | solution.py:23
  71.7 7.2 %collective-permute-start.4 = (f32[34,1]{1,0:T(8,128)S(1)}, f32[34,1]{1,0:T(8,128)S(1)}, u32[]{:S(2)}, u32[]{:S(2)}) collective-permute-start(f32[34,1]{1,0:T(8,128)S(1)} %get-tuple-element.65), channel_id=1, source_target_pairs={{1,0},{2,1},{3,2},{5,4},{6,5},{7,6},{9,8},{10,9},{11,10},{13,12},{... | collective-permute-start | bytes 416 | tf_op jit(solution)/shard_map/ppermute | solution.py:25
  73.1 10.5 %collective-permute-start.6 = (f32[34,1]{1,0:T(8,128)S(1)}, f32[34,1]{1,0:T(8,128)S(1)}, u32[]{:S(2)}, u32[]{:S(2)}) collective-permute-start(f32[34,1]{1,0:T(8,128)S(1)} %get-tuple-element.66), channel_id=1, source_target_pairs={{0,1},{1,2},{2,3},{4,5},{5,6},{6,7},{8,9},{9,10},{10,11},{12,13},{... | collective-permute-start | bytes 416 | tf_op jit(solution)/shard_map/ppermute | solution.py:23
  77.7 6.0 collective-permute-start.5
  79.0 6.0 collective-permute-start.7
  94.4 14.0 %collective-permute-start.13 = (f32[1,64]{1,0:T(1,128)S(1)}, f32[1,64]{1,0:T(1,128)S(1)}, u32[]{:S(2)}, u32[]{:S(2)}) collective-permute-start(f32[1,64]{1,0:T(1,128)S(1)} %get-tuple-element.109), channel_id=1, source_target_pairs={{0,4},{4,8},{8,12},{12,16},{16,20},{20,24},{24,28},{28,32},{32,36}... | collective-permute-start | bytes 776 | tf_op jit(solution)/shard_map/ppermute | solution.py:23
  96.6 11.8 %collective-permute-start.12 = (f32[1,64]{1,0:T(1,128)S(1)}, f32[1,64]{1,0:T(1,128)S(1)}, u32[]{:S(2)}, u32[]{:S(2)}) collective-permute-start(f32[1,64]{1,0:T(1,128)S(1)} %get-tuple-element.110), channel_id=1, source_target_pairs={{4,0},{8,4},{12,8},{16,12},{20,16},{24,20},{28,24},{32,28},{36,32}... | collective-permute-start | bytes 776 | tf_op jit(solution)/shard_map/ppermute | solution.py:25
  108.5 6.0 collective-permute-start.14
  109.8 6.1 collective-permute-start.15
  115.9 7.3 %collective-permute-start.17 = (f32[1,64]{1,0:T(1,128)S(1)}, f32[1,64]{1,0:T(1,128)S(1)}, u32[]{:S(2)}, u32[]{:S(2)}) collective-permute-start(f32[1,64]{1,0:T(1,128)S(1)} %get-tuple-element.107), channel_id=1, source_target_pairs={{0,4},{4,8},{8,12},{12,16},{16,20},{20,24},{24,28},{28,32},{32,36}... | collective-permute-start | bytes 776 | tf_op jit(solution)/shard_map/ppermute | solution.py:23
  126.8 6.1 collective-permute-start.18
  128.1 6.2 collective-permute-start.19
  134.4 8.1 %collective-permute-start.21 = (f32[1,64]{1,0:T(1,128)S(1)}, f32[1,64]{1,0:T(1,128)S(1)}, u32[]{:S(2)}, u32[]{:S(2)}) collective-permute-start(f32[1,64]{1,0:T(1,128)S(1)} %get-tuple-element.105), channel_id=1, source_target_pairs={{0,4},{4,8},{8,12},{12,16},{16,20},{20,24},{24,28},{28,32},{32,36}... | collective-permute-start | bytes 776 | tf_op jit(solution)/shard_map/ppermute | solution.py:23
  142.6 6.3 collective-permute-start.22
  143.9 5.9 collective-permute-start.23
  160.3 6.9 collective-permute-start.26
  161.6 6.4 collective-permute-start.27
  180.7 6.3 collective-permute-start.28
  187.1 6.8 collective-permute-start.30
  188.4 6.3 collective-permute-start.31
  203.0 6.4 collective-permute-start.33
  208.1 5.7 collective-permute-start.32
  213.8 6.9 collective-permute-start.34
  215.1 6.3 collective-permute-start.35
  229.0 5.4 collective-permute-start.37
  233.2 5.4 collective-permute-start.36
  238.6 6.1 collective-permute-start.38
  239.9 6.2 collective-permute-start.39
  246.2 7.0 collective-permute-start.41
  255.9 6.1 collective-permute-start.42
  257.2 6.2 collective-permute-start.43
  263.5 9.5 %collective-permute-start.45 = (f32[1,64]{1,0:T(1,128)S(1)}, f32[1,64]{1,0:T(1,128)S(1)}, u32[]{:S(2)}, u32[]{:S(2)}) collective-permute-start(f32[1,64]{1,0:T(1,128)S(1)} %get-tuple-element.99), channel_id=1, source_target_pairs={{0,4},{4,8},{8,12},{12,16},{16,20},{20,24},{24,28},{28,32},{32,36}... | collective-permute-start | bytes 776 | tf_op jit(solution)/shard_map/ppermute | solution.py:23
  273.0 6.0 collective-permute-start.46
  274.3 6.1 collective-permute-start.47
  283.4 5.7 collective-permute-start.49
  287.8 5.6 collective-permute-start.48
  293.4 6.9 collective-permute-start.50
  294.7 6.4 collective-permute-start.51
  311.2 90.6 %collective-permute-start.53 = (f32[1,128,128]{2,1,0:T(8,128)S(1)}, f32[1,128,128]{2,1,0:T(8,128)S(1)}, u32[]{:S(2)}, u32[]{:S(2)}) collective-permute-start(f32[1,128,128]{2,1,0:T(8,128)S(1)} %get-tuple-element.53), channel_id=1, source_target_pairs={{0,4},{4,8},{8,12},{12,16},{16,20},{20,24},{24,28},{28,32},{32,36}... | collective-permute-start | bytes 196616 | tf_op jit(solution)/shard_map/ppermute | solution.py:23
  315.2 86.6 %collective-permute-start.52 = (f32[1,128,128]{2,1,0:T(8,128)S(1)}, f32[1,128,128]{2,1,0:T(8,128)S(1)}, u32[]{:S(2)}, u32[]{:S(2)}) collective-permute-start(f32[1,128,128]{2,1,0:T(8,128)S(1)} %get-tuple-element.54), channel_id=1, source_target_pairs={{4,0},{8,4},{12,8},{16,12},{20,16},{24,20},{28,24},{32,28},{36,32}... | collective-permute-start | bytes 196616 | tf_op jit(solution)/shard_map/ppermute | solution.py:25
  403.0 6.8 collective-permute-start.54
  404.3 6.3 collective-permute-start.55
  424.6 6.8 collective-permute-start.58
  425.9 6.3 collective-permute-start.59
  447.6 6.1 collective-permute-start.62
  448.9 6.2 collective-permute-start.63
  462.3 6.1 collective-permute-start.66
  463.6 6.2 collective-permute-start.67
  469.9 7.9 %collective-permute-start.69 = (f32[1,64]{1,0:T(1,128)S(1)}, f32[1,64]{1,0:T(1,128)S(1)}, u32[]{:S(2)}, u32[]{:S(2)}) collective-permute-start(f32[1,64]{1,0:T(1,128)S(1)} %get-tuple-element.93), channel_id=1, source_target_pairs={{0,4},{4,8},{8,12},{12,16},{16,20},{20,24},{24,28},{28,32},{32,36}... | collective-permute-start | bytes 776 | tf_op jit(solution)/shard_map/ppermute | solution.py:23
  477.9 5.8 collective-permute-start.70
  479.2 5.9 collective-permute-start.71
  496.3 7.2 %collective-permute-start.74 = (f32[34,1,128]{2,1,0:T(1,128)S(1)}, f32[34,1,128]{2,1,0:T(1,128)S(1)}, u32[]{:S(2)}, u32[]{:S(2)}) collective-permute-start(f32[34,1,128]{2,1,0:T(1,128)S(1)} %get-tuple-element.31), channel_id=1, source_target_pairs={{1,0},{2,1},{3,2},{5,4},{6,5},{7,6},{9,8},{10,9},{11,10},{13,12},{... | collective-permute-start | bytes 52232 | tf_op jit(solution)/shard_map/ppermute | solution.py:25
  497.6 6.4 collective-permute-start.75
  514.2 90.8 %collective-permute-start.77 = (f32[1,128,128]{2,1,0:T(8,128)S(1)}, f32[1,128,128]{2,1,0:T(8,128)S(1)}, u32[]{:S(2)}, u32[]{:S(2)}) collective-permute-start(f32[1,128,128]{2,1,0:T(8,128)S(1)} %get-tuple-element.47), channel_id=1, source_target_pairs={{0,4},{4,8},{8,12},{12,16},{16,20},{20,24},{24,28},{28,32},{32,36}... | collective-permute-start | bytes 196616 | tf_op jit(solution)/shard_map/ppermute | solution.py:23
  518.3 86.7 %collective-permute-start.76 = (f32[1,128,128]{2,1,0:T(8,128)S(1)}, f32[1,128,128]{2,1,0:T(8,128)S(1)}, u32[]{:S(2)}, u32[]{:S(2)}) collective-permute-start(f32[1,128,128]{2,1,0:T(8,128)S(1)} %get-tuple-element.48), channel_id=1, source_target_pairs={{4,0},{8,4},{12,8},{16,12},{20,16},{24,20},{28,24},{32,28},{36,32}... | collective-permute-start | bytes 196616 | tf_op jit(solution)/shard_map/ppermute | solution.py:25
  606.1 6.8 collective-permute-start.78
  607.5 6.3 collective-permute-start.79
  (41 other events, 272.1 us)
where the time goes:
time: 714 us; the launch traced here: 703 us
  blocking collectives  228 us (32%)
  starting transfers between devices  224 us (31%)
  other arithmetic  131 us (18%)
  waiting for transfers between devices  57.2 us (8%)
  matrix products  36.7 us (5%)
  local copies, waits for them, and re-layouts  14.1 us (2%)
  between operations  12.8 us (2%)
    psum x3, blocking collectives, shards(): lax.psum((jnp.sum(residual * u_vec), jnp.sum(w_vec * u_vec)), ('gx', 'gy'))  228 us
    ppermute x40, starting transfers between devices, padded_2(): lax.ppermute(tail, axis, [(i, (i + 1) % count) for i in range(ends)])  172 us
    ppermute x40, starting transfers between devices, padded_2(): lax.ppermute(head, axis, [((i + 1) % count, i) for i in range(ends)])  51.8 us
    ppermute x40, waiting for transfers between devices, padded_2(): lax.ppermute(head, axis, [((i + 1) % count, i) for i in range(ends)])  37.8 us
    dot_general x9, matrix products, line_apply(): jnp.dot(field.reshape(-1, shape[-1]), inverse, precision=lax.Precision.HI...  35.8 us
    reduce_sum x3, other arithmetic, shards(): jnp.sum(w_vec * u_vec)  26.9 us
    another operation x6, other arithmetic, line_inverse(): chol = jnp.linalg.cholesky(matrix)  24.8 us
    reduce_sum x6, other arithmetic, precondition(): target = jnp.sum(coarse, axis=2) / nz  21.5 us
  transfers between devices with their start and end apart: 80, of which 29 were waited for; matrix products, arithmetic and copies ran while one was open for 12% of the time, Pallas kernels for 0%

commit v1 on v0

v1 whole, which is shorter than its diff:
```python
import functools

import jax
import jax.numpy as jnp
from jax import lax
from jax.experimental import pallas as pl
from jax.experimental.pallas import tpu as pltpu
from jax.sharding import PartitionSpec as P


ITERS = 3
SWEEPS = 4
F32 = jnp.float32
BF16 = jnp.bfloat16
MESH = pl.DeviceIdType.MESH
NXL, NY2, NZ = 32, 64, 128
ROWS = 8
SIDES = [(dx, dy) for dx in (-1, 0, 1) for dy in (-1, 0, 1) if (dx, dy) != (0, 0)]


def split_mm(v, w):
    high = v.astype(BF16)
    low = (v - high.astype(F32)).astype(BF16)
    o = jnp.dot(jnp.concatenate([high, low], axis=1), w, preferred_element_type=F32)
    return o[:, :128] + o[:, 128:]


def roll(v, shift, axis):
    return pltpu.roll(v, shift % v.shape[axis], axis)


def line_inverses(coupling, w_refs):
    lane = lax.broadcasted_iota(jnp.int32, (8, 128), 1)
    row = lax.broadcasted_iota(jnp.int32, (8, 128), 0)
    up = jnp.broadcast_to(coupling, (8, 128))
    lo = roll(up, 1, 1)
    factor = jnp.where(row == 0, 1.0, 4.0)
    diag = jnp.where(row == 0, 4.1, 4.4) + factor * (up + lo)
    off_up = factor * up
    off_lo = factor * lo

    def pivots(off, step):
        a, b = diag, -off * off
        c, d = jnp.ones_like(a), jnp.zeros_like(a)
        s = 1
        while s < 128:
            inside = (lane >= s) if step > 0 else (lane < 128 - s)
            ra = jnp.where(inside, roll(a, step * s, 1), 1.0)
            rb = jnp.where(inside, roll(b, step * s, 1), 0.0)
            rc = jnp.where(inside, roll(c, step * s, 1), 0.0)
            rd = jnp.where(inside, roll(d, step * s, 1), 1.0)
            na, nb = a * ra + b * rc, a * rb + b * rd
            nc, nd = c * ra + d * rc, c * rb + d * rd
            inv = 1.0 / na
            a, b, c, d = jnp.ones_like(a), nb * inv, nc * inv, nd * inv
            s *= 2
        return 1.0 / c

    fore = pivots(off_lo, 1)
    back = pivots(off_up, -1)
    main = 1.0 / (fore + back - diag)
    ratio = jnp.where(lane < 127, jnp.log(jnp.maximum(off_up, 1e-30) / fore), 0.0)
    total = jnp.where(lane >= 1, roll(ratio, 1, 1), 0.0)
    s = 1
    while s < 128:
        total = total + jnp.where(lane >= s, roll(total, s, 1), 0.0)
        s *= 2

    r = lax.broadcasted_iota(jnp.int32, (128, 128), 0)
    c = lax.broadcasted_iota(jnp.int32, (128, 128), 1)
    for i, w_ref in enumerate(w_refs):
        def wide(v):
            return jnp.broadcast_to(v[i : i + 1], (128, 128))

        g_row, t_row = wide(main), wide(total)
        g_col, t_col = g_row.T, t_row.T
        g = jnp.where(r <= c, g_row, g_col) * jnp.exp(-jnp.abs(t_row - t_col))
        a_col, u_col = wide(diag).T, wide(off_up).T
        l_col = wide(off_lo).T
        tg = a_col * g - u_col * roll(g, -1, 0) - l_col * roll(g, 1, 0)
        rest = jnp.where(r == c, 1.0, 0.0) - tg
        g = g + jnp.dot(g.astype(BF16), rest.astype(BF16), preferred_element_type=F32)
        high = g.astype(BF16)
        low = (g - high.astype(F32)).astype(BF16)
        both = jnp.concatenate([high, low], axis=1)
        w_ref[...] = jnp.concatenate([both, both], axis=0)


def kernel(
    nx, ny, rhs_ref, mask_ref, coup_ref, x_ref, r_ref,
    inp, outx, outr, fb, ys, rhos, m3, q3, t1s, h1s, hy, sy, w0, w1, kpad,
    blk, nbr, tmat, mn, m2, bars, ybars, nus, red1, red2,
    in_sem, out_sem, sx_sem, rx_sem, sb_sem, rb_sem, s1_sem, r1_sem, s2_sem, r2_sem,
):
    gx, gy = lax.axis_index("gx"), lax.axis_index("gy")
    lo, hi = lax.rem(gx, 4), lax.div(gx, 4)
    ng = nx // 4

    first = [(dl, dg) for dl in range(4) for dg in range(ny) if (dl, dg) != (0, 0)]
    second = list(range(1, ng))

    def first_dev(dl, dg):
        return (hi * 4 + lax.rem(lo + dl, 4), lax.rem(gy + dg, ny))

    def second_dev(dh):
        return (lax.rem(hi + dh, ng) * 4 + lo, gy)

    def side_dev(dx, dy):
        return (lax.rem(gx + dx + nx, nx), lax.rem(gy + dy + ny, ny))

    load = pltpu.make_async_copy(rhs_ref, inp, in_sem)
    load.start()

    def clear(k, carry):
        zero = jnp.zeros((NY2, 128), F32)
        for b in range(2):
            fb[k, 0, b, 8:72, :] = zero
            fb[k, NXL + 1, b, 8:72, :] = zero
        hy[k] = jnp.zeros((2, NXL, 128), F32)
        return carry

    lax.fori_loop(0, 3 * ITERS, clear, 0)
    nbr[...] = jnp.zeros(nbr.shape, F32)

    barrier = pltpu.get_barrier_semaphore()
    for dx, dy in SIDES:
        pl.semaphore_signal(barrier, inc=1, device_id=side_dev(dx, dy), device_id_type=MESH)
    for dl, dg in first:
        pl.semaphore_signal(barrier, inc=1, device_id=first_dev(dl, dg), device_id_type=MESH)
    for dh in second:
        pl.semaphore_signal(barrier, inc=1, device_id=second_dev(dh), device_id_type=MESH)

    kpad[...] = jnp.zeros((1, 128), F32)
    kpad[:, 0:127] = coup_ref[...]
    line_inverses(kpad[...], (w0, w1))

    lane = lax.broadcasted_iota(jnp.int32, (NY2, 128), 1)

    def to_columns(v):
        tmat[...] = jnp.concatenate([v, jnp.zeros((128 - NXL, 128), F32)], axis=0).T

    def expand(dst):
        for b in range(2):
            col = tmat[pl.ds(b, NY2, stride=2), :]
            for x in range(NXL):
                dst[x, b] = jnp.broadcast_to(col[:, x : x + 1], (NY2, 128))

    mask = mask_ref[...].astype(F32)
    blk[0:NXL, :] = mask
    to_columns(mask)
    expand(m3)

    load.wait()

    def start_pass(x, carry):
        acc, means = carry[0], list(carry[1:])
        for b in range(2):
            v = inp[x, pl.ds(b, NY2, stride=2), :]
            m = m3[x, b]
            mean = jnp.sum(v, axis=1, keepdims=True) * (1.0 / NZ)
            means[b] = jnp.where(lane == x, mean, means[b])
            rhos[0, x, b] = m * (v - mean)
            land = (1.0 - m) * v
            acc = acc + jnp.sum((land * land).reshape(8, 8, 128), axis=0)
        return (acc, *means)

    zero = jnp.zeros((NY2, 128), F32)
    nu0, mean0, mean1 = lax.fori_loop(0, NXL, start_pass, (jnp.zeros((8, 128), F32), zero, zero))
    tmat[pl.ds(0, NY2, stride=2), :] = mean0
    tmat[pl.ds(1, NY2, stride=2), :] = mean1
    blk[NXL : 2 * NXL, :] = mask * tmat[...].T[0:NXL]

    pl.semaphore_wait(barrier, len(SIDES) + len(first) + len(second))

    def exists(dx, dy):
        ok = None
        for pos, d, n in ((gx, dx, nx), (gy, dy, ny)):
            if d:
                here = (pos + d >= 0) & (pos + d < n)
                ok = here if ok is None else ok & here
        return ok

    def block_copy(i):
        dx, dy = SIDES[i]
        return pltpu.make_async_remote_copy(
            src_ref=blk, dst_ref=nbr.at[i], send_sem=sb_sem.at[i], recv_sem=rb_sem.at[i],
            device_id=side_dev(dx, dy), device_id_type=MESH,
        )

    for i in range(8):
        pl.when(exists(*SIDES[i]))(lambda i=i: block_copy(i).start())

    def faces(k):
        field = fb.at[k]
        cells = pl.ds(8, NY2)
        ends = (
            (field.at[1, :, cells, :], field.at[NXL + 1, :, cells, :], (-1, 0)),
            (field.at[NXL, :, cells, :], field.at[0, :, cells, :], (1, 0)),
            (sy.at[k, 0], hy.at[k, 1], (0, -1)),
            (sy.at[k, 1], hy.at[k, 0], (0, 1)),
        )
        return [
            (
                pltpu.make_async_remote_copy(
                    src_ref=src, dst_ref=dst, send_sem=sx_sem.at[k, i], recv_sem=rx_sem.at[k, i],
                    device_id=side_dev(*d), device_id_type=MESH,
                ),
                exists(*d), exists(-d[0], -d[1]),
            )
            for i, (src, dst, d) in enumerate(ends)
        ]

    def send(k):
        for copy, there, _ in faces(k):
            pl.when(there)(copy.start)

    def receive(k):
        for copy, there, back in faces(k):
            pl.when(back)(copy.wait_recv)

    def put(k, x, b, v):
        fb[k, x + 1, b, 8:72, :] = v
        if b == 0:
            sy[k, 0, pl.ds(x, 1), :] = v[0:1]
        else:
            sy[k, 1, pl.ds(x, 1), :] = v[NY2 - 1 : NY2]

    def insert(k, x):
        fb[k, x + 1, 1, 7:8, :] = hy[k, 0, pl.ds(x, 1), :]
        fb[k, x + 1, 0, 72:73, :] = hy[k, 1, pl.ds(x, 1), :]

    def stencil(k, x, b):
        mate = fb[k, x + 1, 1 - b, 8:72, :]
        side = fb[k, x + 1, 1 - b, 7:71, :] if b == 0 else fb[k, x + 1, 1 - b, 9:73, :]
        beside = (fb[k, x, b, 8:72, :] + fb[k, x + 2, b, 8:72, :]) + (mate + side)
        return q3[x, b] * fb[k, x + 1, b, 8:72, :], beside

    def tile_sum(v):
        return jnp.sum(v.reshape(8, 8, 128), axis=0)

    def smooth0_pass(i, carry):
        for x8 in range(ROWS):
            x = i * ROWS + x8
            e0 = split_mm(rhos[0, x].reshape(128, 128), w0[...])
            put(0, x, 0, e0[:NY2])
            put(0, x, 1, e0[NY2:])
        return carry

    lax.fori_loop(0, NXL // ROWS, smooth0_pass, 0)
    send(0)

    for i in range(8):
        dx, dy = SIDES[i]
        pl.when(exists(-dx, -dy))(lambda i=i: block_copy(i).wait_recv())

    low_half = lax.broadcasted_iota(jnp.int32, (96, 128), 1) < 64

    def around(rows):
        def column(dy):
            parts = []
            for dx in (-1, 0, 1):
                if (dx, dy) == (0, 0):
                    parts.append(blk[rows, :])
                else:
                    parts.append(nbr[SIDES.index((-dx, -dy)), rows, :])
            return roll(jnp.concatenate(parts, axis=0), 64, 1)

        left, mid, right = column(-1), column(0), column(1)
        return jnp.concatenate(
            [jnp.where(low_half, left, mid), jnp.where(low_half, mid, right)], axis=1
        )

    def local(v):
        a, b = roll(v[32:64, 0:128], 64, 1), roll(v[32:64, 128:256], 64, 1)
        return jnp.where(low_half[:NXL], a, b)

    moves = ((-1, 0), (1, 0), (-1, 1), (1, 1))
    mask2 = around(pl.ds(0, NXL))
    m2[...] = mask2
    bars[0] = around(pl.ds(NXL, NXL))
    open_sides = jnp.zeros((96, 256), F32)
    for i, (s, axis) in enumerate(moves):
        beside = roll(mask2, s, axis)
        mn[i] = beside
        open_sides = open_sides + beside
    to_columns(local(mask2 * (4.0 - open_sides)))
    expand(q3)

    xi = lax.broadcasted_iota(jnp.int32, (96, 256), 0) + (gx * NXL - 32)
    yi = lax.broadcasted_iota(jnp.int32, (96, 256), 1) + (gy * 128 - 64)
    inside = (xi >= 0) & (xi < nx * NXL) & (yi >= 0) & (yi < ny * 128)
    dom = jnp.where(inside, 1.0, 0.0)

    even_x = lax.rem(lax.broadcasted_iota(jnp.int32, (96, 256), 0), 2) == 0
    even_y = lax.rem(lax.broadcasted_iota(jnp.int32, (96, 256), 1), 2) == 0

    def flow(v):
        total = None
        for i, (s, axis) in enumerate(moves):
            term = mn[i] * (roll(v, s, axis) - v)
            total = term if total is None else total + term
        return total

    def mean_step(j):
        m = m2[...]
        e0 = bars[j] * (1.0 / 4.1)
        t = 4.0 * e0 + flow(e0)
        t1 = m * t
        t1 = t1 + jnp.where(even_x, roll(t1, -1, 0), roll(t1, 1, 0))
        t1 = t1 + jnp.where(even_y, roll(t1, -1, 1), roll(t1, 1, 1))
        e1 = t1 * (1.0 / 4.4)
        c = (0.8 / 4.4) * t1
        for _ in range(SWEEPS - 1):
            beside = (roll(c, 2, 0) + roll(c, -2, 0)) + (roll(c, 2, 1) + roll(c, -2, 1))
            c = dom * (c + 0.8 * (t1 - (4.4 * c - beside)) / 4.4)
        f = e1 + c
        rem = m * (t + flow(f) + (e1 - 0.25 * t1) - 0.1 * c)
        d = rem * (1.0 / 4.1)
        ybars[j] = e0 + m * f + d
        bars[j + 1] = m * (4.0 * d + flow(d))

    def coarse_pass(k):
        def body(x2, carry):
            total = None
            for x in (2 * x2, 2 * x2 + 1):
                insert(k, x)
                for b in range(2):
                    own, beside = stencil(k, x, b)
                    t = own + m3[x, b] * beside
                    total = t if total is None else total + t
            t1s[x2] = total
            return carry

        lax.fori_loop(0, NXL // 2, body, 0)

    def correct_pass(k):
        def body(i, carry):
            t1 = t1s[pl.ds(i * 4, 4)].reshape(4 * NY2, 128)
            e1 = split_mm(t1, w1[...])
            h1s[pl.ds(i * 4, 4)] = (0.25 * t1 + 3.0 * e1).reshape(4, NY2, 128)
            for x8 in range(8):
                x = i * 8 + x8
                part = e1[(x8 // 2) * NY2 : (x8 // 2 + 1) * NY2]
                for b in range(2):
                    put(k + 1, x, b, fb[k, x + 1, b, 8:72, :] + m3[x, b] * part)
            return carry

        lax.fori_loop(0, NXL // 8, body, 0)

    def smooth_pass(k, j):
        def body(i, acc):
            for x8 in range(ROWS):
                x = i * ROWS + x8
                insert(k, x)
                rem = []
                for b in range(2):
                    own, beside = stencil(k, x, b)
                    rem.append(own + m3[x, b] * (beside - h1s[lax.div(x, 2)]))
                d = split_mm(jnp.concatenate(rem, axis=0), w0[...])
                for b in range(2):
                    part = d[b * NY2 : (b + 1) * NY2]
                    y = fb[k, x + 1, b, 8:72, :] + part
                    put(k + 1, x, b, part)
                    ys[j, x, b] = y
                    acc = acc + tile_sum(rhos[j, x, b] * y)
            return acc

        return lax.fori_loop(0, NXL // ROWS, body, jnp.zeros((8, 128), F32))

    def next_pass(k, j):
        def body(i, acc):
            for x8 in range(ROWS):
                x = i * ROWS + x8
                insert(k, x)
                new = []
                for b in range(2):
                    own, beside = stencil(k, x, b)
                    v = own + m3[x, b] * beside
                    rhos[j + 1, x, b] = v
                    acc = acc + tile_sum(v * ys[j, x, b])
                    new.append(v)
                if j + 1 < ITERS:
                    e0 = split_mm(jnp.concatenate(new, axis=0), w0[...])
                    put(k + 1, x, 0, e0[:NY2])
                    put(k + 1, x, 1, e0[NY2:])
            return acc

        return lax.fori_loop(0, NXL // ROWS, body, jnp.zeros((8, 128), F32))

    for j in range(ITERS):
        k = 3 * j
        receive(k)
        coarse_pass(k)
        correct_pass(k)
        send(k + 1)
        mean_step(j)
        receive(k + 1)
        acc = smooth_pass(k + 1, j)
        send(k + 2)
        nus[2 * j] = acc + nu0 if j == 0 else acc
        receive(k + 2)
        nus[2 * j + 1] = next_pass(k + 2, j)
        if j + 1 < ITERS:
            send(k + 3)

    rows = lax.broadcasted_iota(jnp.int32, (8, 128), 0)
    part = jnp.zeros((8, 128), F32)
    for n in range(2 * ITERS):
        rho, y = local(bars[(n + 1) // 2]), local(ybars[n // 2])
        v = nus[n] + 128.0 * jnp.sum((rho * y).reshape(4, 8, 128), axis=0)
        part = part + jnp.where(rows == n, jnp.sum(v, axis=0, keepdims=True), 0.0)
    red1[0] = part

    def sum_copies(buf, send_sems, recv_sems, devs):
        return [
            pltpu.make_async_remote_copy(
                src_ref=buf.at[0], dst_ref=buf.at[i + 1], send_sem=send_sems.at[i],
                recv_sem=recv_sems.at[i], device_id=dev, device_id_type=MESH,
            )
            for i, dev in enumerate(devs)
        ]

    def sum_phase(copies, buf):
        for copy in copies:
            copy.start()
        for copy in copies:
            copy.wait_recv()
        total = buf[0]
        for i in range(len(copies)):
            total = total + buf[i + 1]
        return total

    copies1 = sum_copies(red1, s1_sem, r1_sem, [first_dev(*d) for d in first])
    red2[0] = sum_phase(copies1, red1)
    copies2 = sum_copies(red2, s2_sem, r2_sem, [second_dev(d) for d in second])
    total = sum_phase(copies2, red2)
    total = jnp.broadcast_to(jnp.sum(total, axis=1, keepdims=True), (8, 128))
    nu = [total[n : n + 1] for n in range(2 * ITERS)]

    h00, h10, h20 = nu[0] - nu[1], nu[1] - nu[2], nu[2] - nu[3]
    h11, h21, h22 = nu[2] - nu[3], nu[3] - nu[4], nu[4] - nu[5]
    l10, l20 = h10 / h00, h20 / h00
    d1, s21 = h11 - l10 * h10, h21 - l10 * h20
    l21 = s21 / d1
    d2 = h22 - l20 * h20 - l21 * s21
    b1 = nu[1] - l10 * nu[0]
    b2 = nu[2] - l20 * nu[0] - l21 * b1
    c2 = b2 / d2
    c1 = b1 / d1 - l21 * c2
    c0 = nu[0] / h00 - l10 * c1 - l20 * c2
    a0, a1, a2 = 1.0 - c0, c0 - c1, c1 - c2

    xbar = c0 * local(ybars[0]) + c1 * local(ybars[1]) + c2 * local(ybars[2])
    rbar = a1 * local(bars[1]) + a2 * local(bars[2]) + c2 * local(bars[3])
    to_columns(xbar)
    xcols = [tmat[pl.ds(b, NY2, stride=2), :] for b in range(2)]
    to_columns(rbar)
    rcols = [tmat[pl.ds(b, NY2, stride=2), :] for b in range(2)]

    outs = []
    for g in range(4):
        for x in range(8 * g, 8 * g + 8):
            for b in range(2):
                v = inp[x, pl.ds(b, NY2, stride=2), :]
                m = m3[x, b]
                ox = c0 * ys[0, x, b] + c1 * ys[1, x, b] + c2 * ys[2, x, b]
                ox = ox + c0 * ((1.0 - m) * v) + xcols[b][:, x : x + 1]
                orr = a0 * v + a1 * rhos[1, x, b] + a2 * rhos[2, x, b] + c2 * rhos[3, x, b]
                orr = orr + rcols[b][:, x : x + 1]
                outx[x, pl.ds(b, NY2, stride=2), :] = ox
                outr[x, pl.ds(b, NY2, stride=2), :] = orr
        cells = pl.ds(8 * g, 8)
        for i, (src, dst) in enumerate(((outx, x_ref), (outr, r_ref))):
            copy = pltpu.make_async_copy(src.at[cells], dst.at[cells], out_sem.at[i, g])
            copy.start()
            outs.append(copy)

    for i in range(8):
        pl.when(exists(*SIDES[i]))(lambda i=i: block_copy(i).wait_send())
    for k in range(3 * ITERS):
        for copy, there, _ in faces(k):
            pl.when(there)(copy.wait_send)
    for copy in copies1 + copies2:
        copy.wait_send()
    for copy in outs:
        copy.wait()


def shards(nx, ny, right_side, sea_mask, vertical_coupling):
    vmem = pltpu.VMEM
    ng = nx // 4
    n_first = 4 * ny - 1
    out = jax.ShapeDtypeStruct(right_side.shape, F32)
    return pl.pallas_call(
        functools.partial(kernel, nx, ny),
        out_shape=(out, out),
        in_specs=[
            pl.BlockSpec(memory_space=pl.ANY),
            pl.BlockSpec(memory_space=vmem),
            pl.BlockSpec(memory_space=vmem),
        ],
        out_specs=(pl.BlockSpec(memory_space=pl.ANY), pl.BlockSpec(memory_space=pl.ANY)),
        scratch_shapes=[
            vmem((NXL, 128, 128), F32),
            vmem((NXL, 128, 128), F32),
            vmem((NXL, 128, 128), F32),
            vmem((3 * ITERS, NXL + 2, 2, 80, 128), F32),
            vmem((ITERS, NXL, 2, NY2, 128), F32),
            vmem((ITERS + 1, NXL, 2, NY2, 128), F32),
            vmem((NXL, 2, NY2, 128), F32),
            vmem((NXL, 2, NY2, 128), F32),
            vmem((NXL // 2, NY2, 128), F32),
            vmem((NXL // 2, NY2, 128), F32),
            vmem((3 * ITERS, 2, NXL, 128), F32),
            vmem((3 * ITERS, 2, NXL, 128), F32),
            vmem((256, 256), BF16),
            vmem((256, 256), BF16),
            vmem((1, 128), F32),
            vmem((2 * NXL, 128), F32),
            vmem((8, 2 * NXL, 128), F32),
            vmem((128, 128), F32),
            vmem((4, 96, 256), F32),
            vmem((96, 256), F32),
            vmem((ITERS + 1, 96, 256), F32),
            vmem((ITERS, 96, 256), F32),
            vmem((2 * ITERS, 8, 128), F32),
            vmem((n_first + 1, 8, 128), F32),
            vmem((ng, 8, 128), F32),
            pltpu.SemaphoreType.DMA,
            pltpu.SemaphoreType.DMA((2, 4)),
            pltpu.SemaphoreType.DMA((3 * ITERS, 4)),
            pltpu.SemaphoreType.DMA((3 * ITERS, 4)),
            pltpu.SemaphoreType.DMA((8,)),
            pltpu.SemaphoreType.DMA((8,)),
            pltpu.SemaphoreType.DMA((n_first,)),
            pltpu.SemaphoreType.DMA((n_first,)),
            pltpu.SemaphoreType.DMA((ng - 1,)),
            pltpu.SemaphoreType.DMA((ng - 1,)),
        ],
        compiler_params=pltpu.CompilerParams(
            collective_id=0, has_side_effects=True, vmem_limit_bytes=60 * 1024 * 1024
        ),
    )(right_side, sea_mask, vertical_coupling.reshape(1, -1))


def solution(mesh):
    nx, ny = mesh.shape["gx"], mesh.shape["gy"]
    return jax.shard_map(
        functools.partial(shards, nx, ny),
        mesh=mesh,
        in_specs=(P("gx", "gy", None), P("gx", "gy"), P()),
        out_specs=(P("gx", "gy", None), P("gx", "gy", None)),
        check_vma=False,
    )
```

time: 714 us -> 77.9 us (0.11); the launches traced: 703 us -> 77.6 us
  blocking collectives: 228 us -> 0 us
  starting transfers between devices: 224 us -> 0 us
  other arithmetic: 131 us -> 0 us
  Pallas kernels: 0 us -> 72.3 us
  waiting for transfers between devices: 57.2 us -> 0 us
  matrix products: 36.7 us -> 0 us
  between operations: 12.8 us -> 0.65 us
  local copies, waits for them, and re-layouts: 14.1 us -> 4.61 us
    psum x3 -> x0, blocking collectives: 228 us -> none  [shards(): lax.psum((jnp.sum(residual * u_vec), jnp.sum(w_vec * u_vec)), ('gx', 'gy'))]
    ppermute x80 -> x0, starting transfers between devices: 224 us -> none  [the longest x40 172 us: padded_2(): lax.ppermute(tail, axis, [(i, (i + 1) % count) for i in range(ends)])]
    pallas_call x0 -> x1, Pallas kernels: none -> 72.3 us  [shards(): pl.pallas_call(functools.partial(kernel, nx, ny), out_shape=(out, out), i...]
    reduce_sum x12 -> x0, other arithmetic: 58 us -> none  [the longest x3 26.9 us: shards(): jnp.sum(w_vec * u_vec)]
    ppermute x80 -> x0, waiting for transfers between devices: 57.2 us -> none  [the longest x40 37.8 us: padded_2(): lax.ppermute(head, axis, [((i + 1) % count, i) for i in range(ends)])]
    another operation x10 -> x0, other arithmetic: 45.8 us -> none  [the longest x6 24.8 us: line_inverse(): chol = jnp.linalg.cholesky(matrix)]
    dot_general x9 -> x0, matrix products: 35.8 us -> none  [line_apply(): jnp.dot(field.reshape(-1, shape[-1]), inverse, precision=lax.Precision.HI...]
    add x17 -> x0, other arithmetic: 9.32 us -> none  [the longest x1 3.56 us: line_smooth(): maskf[..., None] * line_apply(field, inverse)]
  transfers between devices with their start and end apart: 80 -> 0, of which waited for: 29 -> 0; matrix products, arithmetic and copies ran while one was open for 12% -> 0% of each run, Pallas kernels for 0% -> 0%
where the time goes in v1:
time: 77.9 us; the launch traced here: 77.6 us
  Pallas kernels  72.3 us (93%)
  local copies, waits for them, and re-layouts  4.61 us (6%)
    pallas_call x1, Pallas kernels, shards(): pl.pallas_call(functools.partial(kernel, nx, ny), out_shape=(out, out), i...  72.3 us
    unnamed x4, local copies, waits for them, and re-layouts  4.61 us

profile of v1, /device:TPU:0, one launch (start us, length us, event | category | flops | bytes accessed | tf_op | source)
XLA Modules:
  0.0 77.6 jit_solution(15457295643142043209)
XLA Ops:
  0.6 72.3 %shard_map.50 = (f32[32,128,128]{2,1,0:T(8,128)}, f32[32,128,128]{2,1,0:T(8,128)}) custom-call(f32[32,128,128]{2,1,0:T(8,128)} %rhs_ref.1, s32[32,128]{1,0:T(8,128)} %mask_ref.1, f32[1,127]{1,0:T(1,128)} %bitcast.1), custom_call_target="tpu_custom_call" | custom-call | tf_op jit(solution)/shard_map/pallas_call | solution.py:494
  72.9 0.0 copy-start
  73.0 3.3 %copy.7 = f32[32,128,128]{2,1,0:T(8,128)} copy(f32[32,128,128]{2,1,0:T(8,128)} %get-tuple-element.4) | data formatting | bytes 4194304
  76.2 0.0 copy-done
  76.2 1.3 %copy.8 = f32[32,128,128]{2,1,0:T(8,128)} copy(f32[32,128,128]{2,1,0:T(8,128)S(1)} %copy-done) | data formatting | bytes 4194304
Async XLA Ops:
  72.9 3.3 %copy-start = (f32[32,128,128]{2,1,0:T(8,128)S(1)}, f32[32,128,128]{2,1,0:T(8,128)}, u32[]{:S(2)}) copy-start(f32[32,128,128]{2,1,0:T(8,128)} %get-tuple-element.5) | copy-start | bytes 6291460

commit v2 on v1

--- a/solution.py
+++ b/solution.py
@@ -15,6 +15,7 @@
 MESH = pl.DeviceIdType.MESH
 NXL, NY2, NZ = 32, 64, 128
 ROWS = 8
+HALO = 3
 SIDES = [(dx, dy) for dx in (-1, 0, 1) for dy in (-1, 0, 1) if (dx, dy) != (0, 0)]
 
 
@@ -88,13 +89,15 @@
 
 def kernel(
     nx, ny, rhs_ref, mask_ref, coup_ref, x_ref, r_ref,
-    inp, outx, outr, fb, ys, rhos, m3, q3, t1s, h1s, hy, sy, w0, w1, kpad,
+    inp, outx, outr, rho0, rho1, rho2, rho3, y0, y1, y2, e0b, eb, db, h1s, m3, q3,
+    sr, ss, se0, se, sd, cb0, cb, sm, sq, w0, w1, kpad,
     blk, nbr, tmat, mn, m2, bars, ybars, nus, red1, red2,
     in_sem, out_sem, sx_sem, rx_sem, sb_sem, rb_sem, s1_sem, r1_sem, s2_sem, r2_sem,
 ):
     gx, gy = lax.axis_index("gx"), lax.axis_index("gy")
     lo, hi = lax.rem(gx, 4), lax.div(gx, 4)
     ng = nx // 4
+    rhos, ys = (rho0, rho1, rho2, rho3), (y0, y1, y2)
 
     first = [(dl, dg) for dl in range(4) for dg in range(ny) if (dl, dg) != (0, 0)]
     second = list(range(1, ng))
@@ -111,16 +114,18 @@
     load = pltpu.make_async_copy(rhs_ref, inp, in_sem)
     load.start()
 
-    def clear(k, carry):
-        zero = jnp.zeros((NY2, 128), F32)
-        for b in range(2):
-            fb[k, 0, b, 8:72, :] = zero
-            fb[k, NXL + 1, b, 8:72, :] = zero
-        hy[k] = jnp.zeros((2, NXL, 128), F32)
+    def clear(x, carry):
+        zero = jnp.zeros((2, NY2, 128), F32)
+        for rho in (rho0, rho1, rho2):
+            rho[x] = zero
+            rho[x + NXL + HALO] = zero
         return carry
 
-    lax.fori_loop(0, 3 * ITERS, clear, 0)
+    lax.fori_loop(0, HALO, clear, 0)
+    sr[...] = jnp.zeros(sr.shape, F32)
     nbr[...] = jnp.zeros(nbr.shape, F32)
+    cb0[...] = jnp.zeros(cb0.shape, F32)
+    cb[...] = jnp.zeros(cb.shape, F32)
 
     barrier = pltpu.get_barrier_semaphore()
     for dx, dy in SIDES:
@@ -137,18 +142,37 @@
     lane = lax.broadcasted_iota(jnp.int32, (NY2, 128), 1)
 
     def to_columns(v):
-        tmat[...] = jnp.concatenate([v, jnp.zeros((128 - NXL, 128), F32)], axis=0).T
-
-    def expand(dst):
+        tmat[...] = jnp.concatenate([v, jnp.zeros((128 - v.shape[0], 128), F32)], axis=0).T
+
+    def expand(dst, start, stop, shift):
         for b in range(2):
             col = tmat[pl.ds(b, NY2, stride=2), :]
-            for x in range(NXL):
-                dst[x, b] = jnp.broadcast_to(col[:, x : x + 1], (NY2, 128))
+            for x in range(start, stop):
+                dst[x + shift, b] = jnp.broadcast_to(col[:, x : x + 1], (NY2, 128))
 
     mask = mask_ref[...].astype(F32)
     blk[0:NXL, :] = mask
     to_columns(mask)
-    expand(m3)
+    expand(m3, 0, NXL, 2)
+
+    def put_sides(dst, x, b, v):
+        if b == 0:
+            dst[0, 0, pl.ds(x, 1), :] = v[0:1]
+            dst[0, 2, pl.ds(x, 1), :] = v[1:2]
+            dst[1, 1, pl.ds(x, 1), :] = v[NY2 - 1 : NY2]
+        else:
+            dst[0, 1, pl.ds(x, 1), :] = v[0:1]
+            dst[1, 0, pl.ds(x, 1), :] = v[NY2 - 1 : NY2]
+            dst[1, 2, pl.ds(x, 1), :] = v[NY2 - 2 : NY2 - 1]
+
+    def put(dst, edge, shift, x, b, v):
+        dst[x + shift, b, 8:72, :] = v
+        if edge is not None:
+            row = v[0:1] if b == 0 else v[NY2 - 1 : NY2]
+            edge[b, pl.ds(x + 8, 1), :] = row
+
+    def tile_sum(v):
+        return jnp.sum(v.reshape(8, 8, 128), axis=0)
 
     load.wait()
 
@@ -156,12 +180,14 @@
         acc, means = carry[0], list(carry[1:])
         for b in range(2):
             v = inp[x, pl.ds(b, NY2, stride=2), :]
-            m = m3[x, b]
+            m = m3[x + 2, b]
             mean = jnp.sum(v, axis=1, keepdims=True) * (1.0 / NZ)
             means[b] = jnp.where(lane == x, mean, means[b])
-            rhos[0, x, b] = m * (v - mean)
+            dev = m * (v - mean)
+            rho0[x + HALO, b] = dev
+            put_sides(ss.at[0], x, b, dev)
             land = (1.0 - m) * v
-            acc = acc + jnp.sum((land * land).reshape(8, 8, 128), axis=0)
+            acc = acc + tile_sum(land * land)
         return (acc, *means)
 
     zero = jnp.zeros((NY2, 128), F32)
@@ -181,73 +207,51 @@
         return ok
 
     def block_copy(i):
-        dx, dy = SIDES[i]
         return pltpu.make_async_remote_copy(
             src_ref=blk, dst_ref=nbr.at[i], send_sem=sb_sem.at[i], recv_sem=rb_sem.at[i],
+            device_id=side_dev(*SIDES[i]), device_id_type=MESH,
+        )
+
+    def face(j, i):
+        dx, dy = SIDES[i]
+        if dy == 0:
+            src = rhos[j].at[pl.ds(HALO if dx < 0 else NXL, HALO)]
+            dst = rhos[j].at[pl.ds(NXL + HALO if dx < 0 else 0, HALO)]
+        else:
+            s = 0 if dy < 0 else 1
+            x0, n, to = {-1: (0, 8, 40), 0: (0, NXL, 8), 1: (NXL - 8, 8, 0)}[dx]
+            src = ss.at[j, s, :, pl.ds(x0, n), :]
+            dst = sr.at[j, 1 - s, :, pl.ds(to, n), :]
+        return pltpu.make_async_remote_copy(
+            src_ref=src, dst_ref=dst, send_sem=sx_sem.at[j, i], recv_sem=rx_sem.at[j, i],
             device_id=side_dev(dx, dy), device_id_type=MESH,
         )
 
-    for i in range(8):
+    along_x = [i for i, (dx, dy) in enumerate(SIDES) if dy == 0]
+    along_y = [i for i, (dx, dy) in enumerate(SIDES) if dx == 0]
+    corners = [i for i, (dx, dy) in enumerate(SIDES) if dx and dy]
+
+    def send(j, which):
+        for i in which:
+            pl.when(exists(*SIDES[i]))(lambda i=i: face(j, i).start())
+
+    def receive(j):
+        for i, (dx, dy) in enumerate(SIDES):
+            pl.when(exists(-dx, -dy))(lambda i=i: face(j, i).wait_recv())
+
+    for i in corners + along_x + along_y:
         pl.when(exists(*SIDES[i]))(lambda i=i: block_copy(i).start())
-
-    def faces(k):
-        field = fb.at[k]
-        cells = pl.ds(8, NY2)
-        ends = (
-            (field.at[1, :, cells, :], field.at[NXL + 1, :, cells, :], (-1, 0)),
-            (field.at[NXL, :, cells, :], field.at[0, :, cells, :], (1, 0)),
-            (sy.at[k, 0], hy.at[k, 1], (0, -1)),
-            (sy.at[k, 1], hy.at[k, 0], (0, 1)),
-        )
-        return [
-            (
-                pltpu.make_async_remote_copy(
-                    src_ref=src, dst_ref=dst, send_sem=sx_sem.at[k, i], recv_sem=rx_sem.at[k, i],
-                    device_id=side_dev(*d), device_id_type=MESH,
-                ),
-                exists(*d), exists(-d[0], -d[1]),
-            )
-            for i, (src, dst, d) in enumerate(ends)
-        ]
-
-    def send(k):
-        for copy, there, _ in faces(k):
-            pl.when(there)(copy.start)
-
-    def receive(k):
-        for copy, there, back in faces(k):
-            pl.when(back)(copy.wait_recv)
-
-    def put(k, x, b, v):
-        fb[k, x + 1, b, 8:72, :] = v
-        if b == 0:
-            sy[k, 0, pl.ds(x, 1), :] = v[0:1]
-        else:
-            sy[k, 1, pl.ds(x, 1), :] = v[NY2 - 1 : NY2]
-
-    def insert(k, x):
-        fb[k, x + 1, 1, 7:8, :] = hy[k, 0, pl.ds(x, 1), :]
-        fb[k, x + 1, 0, 72:73, :] = hy[k, 1, pl.ds(x, 1), :]
-
-    def stencil(k, x, b):
-        mate = fb[k, x + 1, 1 - b, 8:72, :]
-        side = fb[k, x + 1, 1 - b, 7:71, :] if b == 0 else fb[k, x + 1, 1 - b, 9:73, :]
-        beside = (fb[k, x, b, 8:72, :] + fb[k, x + 2, b, 8:72, :]) + (mate + side)
-        return q3[x, b] * fb[k, x + 1, b, 8:72, :], beside
-
-    def tile_sum(v):
-        return jnp.sum(v.reshape(8, 8, 128), axis=0)
-
-    def smooth0_pass(i, carry):
+    send(0, along_x + corners + along_y)
+
+    def line_pass0(i, carry):
         for x8 in range(ROWS):
             x = i * ROWS + x8
-            e0 = split_mm(rhos[0, x].reshape(128, 128), w0[...])
-            put(0, x, 0, e0[:NY2])
-            put(0, x, 1, e0[NY2:])
+            e0 = split_mm(rho0[x + HALO].reshape(128, 128), w0[...])
+            put(e0b, cb0, HALO, x, 0, e0[:NY2])
+            put(e0b, cb0, HALO, x, 1, e0[NY2:])
         return carry
 
-    lax.fori_loop(0, NXL // ROWS, smooth0_pass, 0)
-    send(0)
+    lax.fori_loop(0, NXL // ROWS, line_pass0, 0)
 
     for i in range(8):
         dx, dy = SIDES[i]
@@ -271,8 +275,8 @@
         )
 
     def local(v):
-        a, b = roll(v[32:64, 0:128], 64, 1), roll(v[32:64, 128:256], 64, 1)
-        return jnp.where(low_half[:NXL], a, b)
+        a, b = roll(v[:, 0:128], 64, 1), roll(v[:, 128:256], 64, 1)
+        return jnp.where(low_half[: v.shape[0]], a, b)
 
     moves = ((-1, 0), (1, 0), (-1, 1), (1, 1))
     mask2 = around(pl.ds(0, NXL))
@@ -283,8 +287,16 @@
         beside = roll(mask2, s, axis)
         mn[i] = beside
         open_sides = open_sides + beside
-    to_columns(local(mask2 * (4.0 - open_sides)))
-    expand(q3)
+    own2 = mask2 * (4.0 - open_sides)
+    to_columns(local(mask2[24:72]))
+    expand(m3, 6, 8, -6)
+    expand(m3, 40, 42, -6)
+    to_columns(local(own2[24:72]))
+    expand(q3, 6, 42, -6)
+    for a in range(2):
+        for s, at in ((0, 63 - a), (1, 192 + a)):
+            sm[s, a] = jnp.broadcast_to(mask2[24:72, at : at + 1], (48, 128))
+            sq[s, a] = jnp.broadcast_to(own2[24:72, at : at + 1], (48, 128))
 
     xi = lax.broadcasted_iota(jnp.int32, (96, 256), 0) + (gx * NXL - 32)
     yi = lax.broadcasted_iota(jnp.int32, (96, 256), 1) + (gy * 128 - 64)
@@ -293,6 +305,7 @@
 
     even_x = lax.rem(lax.broadcasted_iota(jnp.int32, (96, 256), 0), 2) == 0
     even_y = lax.rem(lax.broadcasted_iota(jnp.int32, (96, 256), 1), 2) == 0
+    even_s = lax.rem(lax.broadcasted_iota(jnp.int32, (48, 128), 0), 2) == 0
 
     def flow(v):
         total = None
@@ -319,94 +332,152 @@
         ybars[j] = e0 + m * f + d
         bars[j + 1] = m * (4.0 * d + flow(d))
 
-    def coarse_pass(k):
-        def body(x2, carry):
-            total = None
-            for x in (2 * x2, 2 * x2 + 1):
-                insert(k, x)
-                for b in range(2):
-                    own, beside = stencil(k, x, b)
-                    t = own + m3[x, b] * beside
-                    total = t if total is None else total + t
-            t1s[x2] = total
+    def insert(dst, src, shift, x):
+        dst[x + shift, 1, 7:8, :] = src[0, pl.ds(x + 8, 1), :]
+        dst[x + shift, 0, 72:73, :] = src[1, pl.ds(x + 8, 1), :]
+
+    def stencil(src, shift, x, b, less=None):
+        mate = src[x + shift, 1 - b, 8:72, :]
+        side = src[x + shift, 1 - b, 7:71, :] if b == 0 else src[x + shift, 1 - b, 9:73, :]
+        beside = (src[x + shift - 1, b, 8:72, :] + src[x + shift + 1, b, 8:72, :]) + (mate + side)
+        if less is not None:
+            beside = beside - less
+        return q3[x + 2, b] * src[x + shift, b, 8:72, :] + m3[x + 2, b] * beside
+
+    def strip_beside(v):
+        return roll(v, 1, 0) + roll(v, -1, 0)
+
+    def halo_lines(j):
+        for x in (-3, -2, -1, 32, 33, 34):
+            e0 = split_mm(rhos[j][x + HALO].reshape(128, 128), w0[...])
+            put(e0b, cb0, HALO, x, 0, e0[:NY2])
+            put(e0b, cb0, HALO, x, 1, e0[NY2:])
+        se0[...] = split_mm(sr[j].reshape(288, 128), w0[...]).reshape(2, 3, 48, 128)
+
+    def strip_correct():
+        t1 = []
+        for s in range(2):
+            near, mid, far = se0[s, 0], se0[s, 1], se0[s, 2]
+            t = sq[s, 0] * near + sm[s, 0] * (cb0[s] + mid + strip_beside(near))
+            t = t + sq[s, 1] * mid + sm[s, 1] * (near + far + strip_beside(mid))
+            t1.append(t + jnp.where(even_s, roll(t, -1, 0), roll(t, 1, 0)))
+        t1 = jnp.concatenate(t1, axis=0)
+        e1 = split_mm(t1, w1[...])
+        h1 = 0.25 * t1 + 3.0 * e1
+        for s in range(2):
+            part = e1[48 * s : 48 * s + 48]
+            for a in range(2):
+                se[s, a] = se0[s, a] + sm[s, a] * part
+            sd[s] = h1[48 * s : 48 * s + 48]
+
+    def strip_smooth():
+        rem = []
+        for s in range(2):
+            near, far = se[s, 0], se[s, 1]
+            rem.append(sq[s, 0] * near + sm[s, 0] * (cb[s] + far + strip_beside(near) - sd[s]))
+        sd[...] = split_mm(jnp.concatenate(rem, axis=0), w0[...]).reshape(2, 48, 128)
+
+    def correct_pass():
+        def body(i, carry):
+            t1 = []
+            for k in range(6):
+                x2 = i * 6 + k
+                total = None
+                for x in (2 * x2 - 2, 2 * x2 - 1):
+                    insert(e0b, se0.at[:, 0], HALO, x)
+                    for b in range(2):
+                        t = stencil(e0b, HALO, x, b)
+                        total = t if total is None else total + t
+                t1.append(total)
+            t1 = jnp.concatenate(t1, axis=0)
+            e1 = split_mm(t1, w1[...])
+            h1s[pl.ds(i * 6, 6)] = (0.25 * t1 + 3.0 * e1).reshape(6, NY2, 128)
+            for k in range(6):
+                x2 = i * 6 + k
+                part = e1[k * NY2 : (k + 1) * NY2]
+                for x in (2 * x2 - 2, 2 * x2 - 1):
+                    for b in range(2):
+                        v = e0b[x + HALO, b, 8:72, :] + m3[x + 2, b] * part
+                        put(eb, cb, HALO, x, b, v)
             return carry
 
-        lax.fori_loop(0, NXL // 2, body, 0)
-
-    def correct_pass(k):
-        def body(i, carry):
-            t1 = t1s[pl.ds(i * 4, 4)].reshape(4 * NY2, 128)
-            e1 = split_mm(t1, w1[...])
-            h1s[pl.ds(i * 4, 4)] = (0.25 * t1 + 3.0 * e1).reshape(4, NY2, 128)
-            for x8 in range(8):
-                x = i * 8 + x8
-                part = e1[(x8 // 2) * NY2 : (x8 // 2 + 1) * NY2]
-                for b in range(2):
-                    put(k + 1, x, b, fb[k, x + 1, b, 8:72, :] + m3[x, b] * part)
-            return carry
-
-        lax.fori_loop(0, NXL // 8, body, 0)
-
-    def smooth_pass(k, j):
+        lax.fori_loop(0, 3, body, 0)
+
+    def smooth_row(x, half):
+        insert(eb, se.at[:, 0], HALO, x)
+        rem = [stencil(eb, HALO, x, b, h1s[half + 1]) for b in range(2)]
+        return split_mm(jnp.concatenate(rem, axis=0), w0[...])
+
+    def smooth_pass(j):
+        for x, half in ((-1, -1), (NXL, NXL // 2)):
+            d = smooth_row(x, half)
+            for b in range(2):
+                put(db, None, 1, x, b, d[b * NY2 : (b + 1) * NY2])
+
         def body(i, acc):
             for x8 in range(ROWS):
                 x = i * ROWS + x8
-                insert(k, x)
-                rem = []
-                for b in range(2):
-                    own, beside = stencil(k, x, b)
-                    rem.append(own + m3[x, b] * (beside - h1s[lax.div(x, 2)]))
-                d = split_mm(jnp.concatenate(rem, axis=0), w0[...])
+                d = smooth_row(x, i * (ROWS // 2) + x8 // 2)
                 for b in range(2):
                     part = d[b * NY2 : (b + 1) * NY2]
-                    y = fb[k, x + 1, b, 8:72, :] + part
-                    put(k + 1, x, b, part)
-                    ys[j, x, b] = y
-                    acc = acc + tile_sum(rhos[j, x, b] * y)
+                    y = eb[x + HALO, b, 8:72, :] + part
+                    put(db, None, 1, x, b, part)
+                    ys[j][x, b] = y
+                    acc = acc + tile_sum(rhos[j][x + HALO, b] * y)
             return acc
 
         return lax.fori_loop(0, NXL // ROWS, body, jnp.zeros((8, 128), F32))
 
-    def next_pass(k, j):
-        def body(i, acc):
+    def next_pass(j):
+        shift = HALO if j + 1 < ITERS else 0
+
+        def rows(i, acc):
             for x8 in range(ROWS):
                 x = i * ROWS + x8
-                insert(k, x)
+                insert(db, sd, 1, x)
                 new = []
                 for b in range(2):
-                    own, beside = stencil(k, x, b)
-                    v = own + m3[x, b] * beside
-                    rhos[j + 1, x, b] = v
-                    acc = acc + tile_sum(v * ys[j, x, b])
+                    v = stencil(db, 1, x, b)
+                    rhos[j + 1][x + shift, b] = v
+                    acc = acc + tile_sum(v * ys[j][x, b])
                     new.append(v)
+                    if j + 1 < ITERS:
+                        put_sides(ss.at[j + 1], x, b, v)
                 if j + 1 < ITERS:
                     e0 = split_mm(jnp.concatenate(new, axis=0), w0[...])
-                    put(k + 1, x, 0, e0[:NY2])
-                    put(k + 1, x, 1, e0[NY2:])
+                    put(e0b, cb0, HALO, x, 0, e0[:NY2])
+                    put(e0b, cb0, HALO, x, 1, e0[NY2:])
             return acc
 
-        return lax.fori_loop(0, NXL // ROWS, body, jnp.zeros((8, 128), F32))
+        last = NXL // ROWS - 1
+        acc = lax.fori_loop(0, 2, lambda i, a: rows(i * last, a), jnp.zeros((8, 128), F32))
+        if j + 1 < ITERS:
+            send(j + 1, along_x + corners)
+        acc = lax.fori_loop(1, last, rows, acc)
+        if j + 1 < ITERS:
+            send(j + 1, along_y)
+        return acc
 
     for j in range(ITERS):
-        k = 3 * j
-        receive(k)
-        coarse_pass(k)
-        correct_pass(k)
-        send(k + 1)
-        mean_step(j)
-        receive(k + 1)
-        acc = smooth_pass(k + 1, j)
-        send(k + 2)
+        receive(j)
+        halo_lines(j)
+        strip_correct()
+        correct_pass()
+        strip_smooth()
+        acc = smooth_pass(j)
         nus[2 * j] = acc + nu0 if j == 0 else acc
-        receive(k + 2)
-        nus[2 * j + 1] = next_pass(k + 2, j)
-        if j + 1 < ITERS:
-            send(k + 3)
+        nus[2 * j + 1] = next_pass(j)
+        if j == 0:
+            mean_step(0)
+            mean_step(1)
+        if j == 1:
+            mean_step(2)
 
     rows = lax.broadcasted_iota(jnp.int32, (8, 128), 0)
     part = jnp.zeros((8, 128), F32)
+    here = pl.ds(32, NXL)
     for n in range(2 * ITERS):
-        rho, y = local(bars[(n + 1) // 2]), local(ybars[n // 2])
+        rho, y = local(bars[(n + 1) // 2, here]), local(ybars[n // 2, here])
         v = nus[n] + 128.0 * jnp.sum((rho * y).reshape(4, 8, 128), axis=0)
         part = part + jnp.where(rows == n, jnp.sum(v, axis=0, keepdims=True), 0.0)
     red1[0] = part
@@ -450,8 +521,8 @@
     c0 = nu[0] / h00 - l10 * c1 - l20 * c2
     a0, a1, a2 = 1.0 - c0, c0 - c1, c1 - c2
 
-    xbar = c0 * local(ybars[0]) + c1 * local(ybars[1]) + c2 * local(ybars[2])
-    rbar = a1 * local(bars[1]) + a2 * local(bars[2]) + c2 * local(bars[3])
+    xbar = c0 * local(ybars[0, here]) + c1 * local(ybars[1, here]) + c2 * local(ybars[2, here])
+    rbar = a1 * local(bars[1, here]) + a2 * local(bars[2, here]) + c2 * local(bars[3, here])
     to_columns(xbar)
     xcols = [tmat[pl.ds(b, NY2, stride=2), :] for b in range(2)]
     to_columns(rbar)
@@ -462,10 +533,10 @@
         for x in range(8 * g, 8 * g + 8):
             for b in range(2):
                 v = inp[x, pl.ds(b, NY2, stride=2), :]
-                m = m3[x, b]
-                ox = c0 * ys[0, x, b] + c1 * ys[1, x, b] + c2 * ys[2, x, b]
+                m = m3[x + 2, b]
+                ox = c0 * y0[x, b] + c1 * y1[x, b] + c2 * y2[x, b]
                 ox = ox + c0 * ((1.0 - m) * v) + xcols[b][:, x : x + 1]
-                orr = a0 * v + a1 * rhos[1, x, b] + a2 * rhos[2, x, b] + c2 * rhos[3, x, b]
+                orr = a0 * v + a1 * rho1[x + HALO, b] + a2 * rho2[x + HALO, b] + c2 * rho3[x, b]
                 orr = orr + rcols[b][:, x : x + 1]
                 outx[x, pl.ds(b, NY2, stride=2), :] = ox
                 outr[x, pl.ds(b, NY2, stride=2), :] = orr
@@ -477,9 +548,8 @@
 
     for i in range(8):
         pl.when(exists(*SIDES[i]))(lambda i=i: block_copy(i).wait_send())
-    for k in range(3 * ITERS):
-        for copy, there, _ in faces(k):
-            pl.when(there)(copy.wait_send)
+        for j in range(ITERS):
+            pl.when(exists(*SIDES[i]))(lambda i=i, j=j: face(j, i).wait_send())
     for copy in copies1 + copies2:
         copy.wait_send()
     for copy in outs:
@@ -504,15 +574,28 @@
             vmem((NXL, 128, 128), F32),
             vmem((NXL, 128, 128), F32),
             vmem((NXL, 128, 128), F32),
-            vmem((3 * ITERS, NXL + 2, 2, 80, 128), F32),
-            vmem((ITERS, NXL, 2, NY2, 128), F32),
-            vmem((ITERS + 1, NXL, 2, NY2, 128), F32),
+            vmem((NXL + 2 * HALO, 2, NY2, 128), F32),
+            vmem((NXL + 2 * HALO, 2, NY2, 128), F32),
+            vmem((NXL + 2 * HALO, 2, NY2, 128), F32),
             vmem((NXL, 2, NY2, 128), F32),
             vmem((NXL, 2, NY2, 128), F32),
-            vmem((NXL // 2, NY2, 128), F32),
-            vmem((NXL // 2, NY2, 128), F32),
-            vmem((3 * ITERS, 2, NXL, 128), F32),
-            vmem((3 * ITERS, 2, NXL, 128), F32),
+            vmem((NXL, 2, NY2, 128), F32),
+            vmem((NXL, 2, NY2, 128), F32),
+            vmem((NXL + 2 * HALO, 2, 80, 128), F32),
+            vmem((NXL + 2 * HALO, 2, 80, 128), F32),
+            vmem((NXL + 2, 2, 80, 128), F32),
+            vmem((NXL // 2 + 2, NY2, 128), F32),
+            vmem((NXL + 4, 2, NY2, 128), F32),
+            vmem((NXL + 4, 2, NY2, 128), F32),
+            vmem((ITERS, 2, 3, 48, 128), F32),
+            vmem((ITERS, 2, 3, NXL, 128), F32),
+            vmem((2, 3, 48, 128), F32),
+            vmem((2, 2, 48, 128), F32),
+            vmem((2, 48, 128), F32),
+            vmem((2, 48, 128), F32),
+            vmem((2, 48, 128), F32),
+            vmem((2, 2, 48, 128), F32),
+            vmem((2, 2, 48, 128), F32),
             vmem((256, 256), BF16),
             vmem((256, 256), BF16),
             vmem((1, 128), F32),
@@ -528,8 +611,8 @@
             vmem((ng, 8, 128), F32),
             pltpu.SemaphoreType.DMA,
             pltpu.SemaphoreType.DMA((2, 4)),
-            pltpu.SemaphoreType.DMA((3 * ITERS, 4)),
-            pltpu.SemaphoreType.DMA((3 * ITERS, 4)),
+            pltpu.SemaphoreType.DMA((ITERS, 8)),
+            pltpu.SemaphoreType.DMA((ITERS, 8)),
             pltpu.SemaphoreType.DMA((8,)),
             pltpu.SemaphoreType.DMA((8,)),
             pltpu.SemaphoreType.DMA((n_first,)),

time: 77.9 us -> 58.2 us (0.75)
  Pallas kernels: 72.3 us -> 52.6 us
    pallas_call x1, Pallas kernels: 72.3 us -> 52.6 us  [shards(): pl.pallas_call(functools.partial(kernel, nx, ny), out_shape=(out, out), i...]
where the time goes in v2:
time: 58.2 us; the launch traced here: 57.9 us
  Pallas kernels  52.6 us (90%)
  local copies, waits for them, and re-layouts  4.61 us (8%)
  between operations  0.65 us (1%)
    pallas_call x1, Pallas kernels, shards(): pl.pallas_call(functools.partial(kernel, nx, ny), out_shape=(out, out), i...  52.6 us
    unnamed x4, local copies, waits for them, and re-layouts  4.61 us

profile of v2, /device:TPU:0, one launch (start us, length us, event | category | flops | bytes accessed | tf_op | source)
XLA Modules:
  0.0 57.9 jit_solution(8462206252866549212)
XLA Ops:
  0.6 52.6 %shard_map.50 = (f32[32,128,128]{2,1,0:T(8,128)}, f32[32,128,128]{2,1,0:T(8,128)}) custom-call(f32[32,128,128]{2,1,0:T(8,128)} %rhs_ref.1, s32[32,128]{1,0:T(8,128)} %mask_ref.1, f32[1,127]{1,0:T(1,128)} %bitcast.1), custom_call_target="tpu_custom_call" | custom-call | tf_op jit(solution)/shard_map/pallas_call | solution.py:564
  53.3 0.0 copy-start
  53.3 3.3 %copy.7 = f32[32,128,128]{2,1,0:T(8,128)} copy(f32[32,128,128]{2,1,0:T(8,128)} %get-tuple-element.4) | data formatting | bytes 4194304
  56.5 0.0 copy-done
  56.5 1.3 %copy.8 = f32[32,128,128]{2,1,0:T(8,128)} copy(f32[32,128,128]{2,1,0:T(8,128)S(1)} %copy-done) | data formatting | bytes 4194304
Async XLA Ops:
  53.3 3.3 %copy-start = (f32[32,128,128]{2,1,0:T(8,128)S(1)}, f32[32,128,128]{2,1,0:T(8,128)}, u32[]{:S(2)}) copy-start(f32[32,128,128]{2,1,0:T(8,128)} %get-tuple-element.5) | copy-start | bytes 6291460

commit v3 on v2

--- a/solution.py
+++ b/solution.py
@@ -1,4 +1,6 @@
 import functools
+import itertools
+import math
 
 import jax
 import jax.numpy as jnp
@@ -16,6 +18,8 @@
 NXL, NY2, NZ = 32, 64, 128
 ROWS = 8
 HALO = 3
+H = 32
+PHASES = ("cz", "xy")
 SIDES = [(dx, dy) for dx in (-1, 0, 1) for dy in (-1, 0, 1) if (dx, dy) != (0, 0)]
 
 
@@ -88,30 +92,41 @@
 
 
 def kernel(
-    nx, ny, rhs_ref, mask_ref, coup_ref, x_ref, r_ref,
-    inp, outx, outr, rho0, rho1, rho2, rho3, y0, y1, y2, e0b, eb, db, h1s, m3, q3,
+    nx, ny, rhs_ref, mask_hbm, coup_hbm, x_ref, r_ref,
+    mask_ref, coup_ref, inp, rho0, rho1, rho2, rho3, y0, y1, y2, e0b, eb, db, h1s, m3, q3,
     sr, ss, se0, se, sd, cb0, cb, sm, sq, w0, w1, kpad,
-    blk, nbr, tmat, mn, m2, bars, ybars, nus, red1, red2,
-    in_sem, out_sem, sx_sem, rx_sem, sb_sem, rb_sem, s1_sem, r1_sem, s2_sem, r2_sem,
+    blk, nbr, tmat, mn, m2, bars, ybars, nus, red0, red1, red2,
+    in_sem, sx_sem, rx_sem, sb_sem, rb_sem, ss_sem, rs_sem,
 ):
     gx, gy = lax.axis_index("gx"), lax.axis_index("gy")
-    lo, hi = lax.rem(gx, 4), lax.div(gx, 4)
-    ng = nx // 4
+    reds = (red0, red1, red2)
     rhos, ys = (rho0, rho1, rho2, rho3), (y0, y1, y2)
 
-    first = [(dl, dg) for dl in range(4) for dg in range(ny) if (dl, dg) != (0, 0)]
-    second = list(range(1, ng))
-
-    def first_dev(dl, dg):
-        return (hi * 4 + lax.rem(lo + dl, 4), lax.rem(gy + dg, ny))
-
-    def second_dev(dh):
-        return (lax.rem(hi + dh, ng) * 4 + lo, gy)
+    sizes = {"x": nx // 8, "y": 4, "c": 2, "z": ny}
+    place = {"x": lax.div(gx, 8), "y": lax.rem(lax.div(gx, 2), 4), "c": lax.rem(gx, 2), "z": gy}
+
+    def partners(axes):
+        devs = []
+        for steps in itertools.product(*(range(sizes[axis]) for axis in axes)):
+            if any(steps):
+                at = dict(place)
+                for axis, step in zip(axes, steps):
+                    at[axis] = lax.rem(place[axis] + step, sizes[axis])
+                devs.append((at["x"] * 8 + at["y"] * 2 + at["c"], at["z"]))
+        return devs
+
+    phases = [partners(axes) for axes in PHASES]
 
     def side_dev(dx, dy):
         return (lax.rem(gx + dx + nx, nx), lax.rem(gy + dy + ny, ny))
 
-    load = pltpu.make_async_copy(rhs_ref, inp, in_sem)
+    small = [
+        pltpu.make_async_copy(coup_hbm, coup_ref, in_sem.at[0]),
+        pltpu.make_async_copy(mask_hbm, mask_ref, in_sem.at[1]),
+    ]
+    load = pltpu.make_async_copy(rhs_ref, inp, in_sem.at[2])
+    for copy in small:
+        copy.start()
     load.start()
 
     def clear(x, carry):
@@ -130,14 +145,13 @@
     barrier = pltpu.get_barrier_semaphore()
     for dx, dy in SIDES:
         pl.semaphore_signal(barrier, inc=1, device_id=side_dev(dx, dy), device_id_type=MESH)
-    for dl, dg in first:
-        pl.semaphore_signal(barrier, inc=1, device_id=first_dev(dl, dg), device_id_type=MESH)
-    for dh in second:
-        pl.semaphore_signal(barrier, inc=1, device_id=second_dev(dh), device_id_type=MESH)
-
+    for dev in sum(phases, []):
+        pl.semaphore_signal(barrier, inc=1, device_id=dev, device_id_type=MESH)
+
+    for copy in small:
+        copy.wait()
     kpad[...] = jnp.zeros((1, 128), F32)
     kpad[:, 0:127] = coup_ref[...]
-    line_inverses(kpad[...], (w0, w1))
 
     lane = lax.broadcasted_iota(jnp.int32, (NY2, 128), 1)
 
@@ -155,30 +169,29 @@
     to_columns(mask)
     expand(m3, 0, NXL, 2)
 
-    def put_sides(dst, x, b, v):
-        if b == 0:
-            dst[0, 0, pl.ds(x, 1), :] = v[0:1]
-            dst[0, 2, pl.ds(x, 1), :] = v[1:2]
-            dst[1, 1, pl.ds(x, 1), :] = v[NY2 - 1 : NY2]
-        else:
-            dst[0, 1, pl.ds(x, 1), :] = v[0:1]
-            dst[1, 0, pl.ds(x, 1), :] = v[NY2 - 1 : NY2]
-            dst[1, 2, pl.ds(x, 1), :] = v[NY2 - 2 : NY2 - 1]
-
-    def put(dst, edge, shift, x, b, v):
-        dst[x + shift, b, 8:72, :] = v
-        if edge is not None:
-            row = v[0:1] if b == 0 else v[NY2 - 1 : NY2]
+    def put_sides(dst, x, b, v, h=None):
+        n = v.shape[0]
+        for half, d, row in (
+            ((0, 0, 0), (0, 2, 1), (1, 1, n - 1)) if b == 0 else ((0, 1, 0), (1, 0, n - 1), (1, 2, n - 2))
+        ):
+            if h in (None, half):
+                dst[half, d, pl.ds(x, 1), :] = v[row : row + 1]
+
+    def put(dst, edge, shift, x, b, v, h=None):
+        y0, n = (8, NY2) if h is None else (8 + H * h, H)
+        dst[x + shift, b, y0 : y0 + n, :] = v
+        if edge is not None and h in (None, b):
+            row = v[0:1] if b == 0 else v[n - 1 : n]
             edge[b, pl.ds(x + 8, 1), :] = row
 
     def tile_sum(v):
-        return jnp.sum(v.reshape(8, 8, 128), axis=0)
+        return jnp.sum(v.reshape(-1, 8, 128), axis=0)
 
     load.wait()
 
-    def start_pass(x, carry):
+    def start_pass(i, carry):
         acc, means = carry[0], list(carry[1:])
-        for b in range(2):
+        for x, b in [(i * 4 + k, b) for k in range(4) for b in range(2)]:
             v = inp[x, pl.ds(b, NY2, stride=2), :]
             m = m3[x + 2, b]
             mean = jnp.sum(v, axis=1, keepdims=True) * (1.0 / NZ)
@@ -191,12 +204,12 @@
         return (acc, *means)
 
     zero = jnp.zeros((NY2, 128), F32)
-    nu0, mean0, mean1 = lax.fori_loop(0, NXL, start_pass, (jnp.zeros((8, 128), F32), zero, zero))
+    nu0, mean0, mean1 = lax.fori_loop(0, NXL // 4, start_pass, (jnp.zeros((8, 128), F32), zero, zero))
     tmat[pl.ds(0, NY2, stride=2), :] = mean0
     tmat[pl.ds(1, NY2, stride=2), :] = mean1
     blk[NXL : 2 * NXL, :] = mask * tmat[...].T[0:NXL]
 
-    pl.semaphore_wait(barrier, len(SIDES) + len(first) + len(second))
+    pl.semaphore_wait(barrier, len(SIDES) + sum(map(len, phases)))
 
     def exists(dx, dy):
         ok = None
@@ -242,6 +255,7 @@
     for i in corners + along_x + along_y:
         pl.when(exists(*SIDES[i]))(lambda i=i: block_copy(i).start())
     send(0, along_x + corners + along_y)
+    line_inverses(kpad[...], (w0, w1))
 
     def line_pass0(i, carry):
         for x8 in range(ROWS):
@@ -336,13 +350,29 @@
         dst[x + shift, 1, 7:8, :] = src[0, pl.ds(x + 8, 1), :]
         dst[x + shift, 0, 72:73, :] = src[1, pl.ds(x + 8, 1), :]
 
-    def stencil(src, shift, x, b, less=None):
-        mate = src[x + shift, 1 - b, 8:72, :]
-        side = src[x + shift, 1 - b, 7:71, :] if b == 0 else src[x + shift, 1 - b, 9:73, :]
-        beside = (src[x + shift - 1, b, 8:72, :] + src[x + shift + 1, b, 8:72, :]) + (mate + side)
-        if less is not None:
-            beside = beside - less
-        return q3[x + 2, b] * src[x + shift, b, 8:72, :] + m3[x + 2, b] * beside
+    def stencil_rows(src, shift, x0, count, less=None):
+        out = {}
+        for h in range(2):
+            y0 = 8 + H * h
+            held = {}
+
+            def centre(x, b):
+                if (x, b) not in held:
+                    held[x, b] = src[x0 + x + shift, b, y0 : y0 + H, :]
+                return held[x, b]
+
+            for x in range(count):
+                minus = None if less is None else less(x, h)
+                for b in range(2):
+                    at = y0 - 1 if b == 0 else y0 + 1
+                    beside = centre(x, 1 - b) + src[x0 + x + shift, 1 - b, at : at + H, :]
+                    beside = beside + (centre(x - 1, b) + centre(x + 1, b))
+                    if minus is not None:
+                        beside = beside - minus
+                    q = q3[x0 + x + 2, b, H * h : H * h + H, :]
+                    m = m3[x0 + x + 2, b, H * h : H * h + H, :]
+                    out[x, h, b] = q * centre(x, b) + m * beside
+        return out
 
     def strip_beside(v):
         return roll(v, 1, 0) + roll(v, -1, 0)
@@ -379,51 +409,54 @@
 
     def correct_pass():
         def body(i, carry):
-            t1 = []
-            for k in range(6):
-                x2 = i * 6 + k
-                total = None
-                for x in (2 * x2 - 2, 2 * x2 - 1):
-                    insert(e0b, se0.at[:, 0], HALO, x)
+            x0 = i * 12 - 2
+            for x in range(12):
+                insert(e0b, se0.at[:, 0], HALO, x0 + x)
+            t = stencil_rows(e0b, HALO, x0, 12)
+            keys = [(k, h) for h in range(2) for k in range(6)]
+            t1 = jnp.concatenate(
+                [
+                    (t[2 * k, h, 0] + t[2 * k, h, 1]) + (t[2 * k + 1, h, 0] + t[2 * k + 1, h, 1])
+                    for k, h in keys
+                ],
+                axis=0,
+            )
+            e1 = split_mm(t1, w1[...])
+            h1 = 0.25 * t1 + 3.0 * e1
+            for n, (k, h) in enumerate(keys):
+                part = e1[n * H : n * H + H]
+                h1s[i * 6 + k, h * H : h * H + H, :] = h1[n * H : n * H + H]
+                for x in (2 * k, 2 * k + 1):
                     for b in range(2):
-                        t = stencil(e0b, HALO, x, b)
-                        total = t if total is None else total + t
-                t1.append(total)
-            t1 = jnp.concatenate(t1, axis=0)
-            e1 = split_mm(t1, w1[...])
-            h1s[pl.ds(i * 6, 6)] = (0.25 * t1 + 3.0 * e1).reshape(6, NY2, 128)
-            for k in range(6):
-                x2 = i * 6 + k
-                part = e1[k * NY2 : (k + 1) * NY2]
-                for x in (2 * x2 - 2, 2 * x2 - 1):
-                    for b in range(2):
-                        v = e0b[x + HALO, b, 8:72, :] + m3[x + 2, b] * part
-                        put(eb, cb, HALO, x, b, v)
+                        m = m3[x0 + x + 2, b, h * H : h * H + H, :]
+                        e0 = e0b[x0 + x + HALO, b, 8 + h * H : 8 + h * H + H, :]
+                        put(eb, cb, HALO, x0 + x, b, e0 + m * part, h)
             return carry
 
         lax.fori_loop(0, 3, body, 0)
 
-    def smooth_row(x, half):
-        insert(eb, se.at[:, 0], HALO, x)
-        rem = [stencil(eb, HALO, x, b, h1s[half + 1]) for b in range(2)]
-        return split_mm(jnp.concatenate(rem, axis=0), w0[...])
+    def smooth_rows(x0, count, half0):
+        for x in range(count):
+            insert(eb, se.at[:, 0], HALO, x0 + x)
+        rem = stencil_rows(
+            eb, HALO, x0, count,
+            lambda x, h: h1s[half0 + x // 2 + 1, h * H : h * H + H, :],
+        )
+        d = split_mm(jnp.concatenate(list(rem.values()), axis=0), w0[...])
+        return [(key, d[n * H : n * H + H]) for n, key in enumerate(rem)]
 
     def smooth_pass(j):
-        for x, half in ((-1, -1), (NXL, NXL // 2)):
-            d = smooth_row(x, half)
-            for b in range(2):
-                put(db, None, 1, x, b, d[b * NY2 : (b + 1) * NY2])
+        for x0, half0 in ((-1, -1), (NXL, NXL // 2)):
+            for (x, h, b), d in smooth_rows(x0, 1, half0):
+                put(db, None, 1, x0 + x, b, d, h)
 
         def body(i, acc):
-            for x8 in range(ROWS):
-                x = i * ROWS + x8
-                d = smooth_row(x, i * (ROWS // 2) + x8 // 2)
-                for b in range(2):
-                    part = d[b * NY2 : (b + 1) * NY2]
-                    y = eb[x + HALO, b, 8:72, :] + part
-                    put(db, None, 1, x, b, part)
-                    ys[j][x, b] = y
-                    acc = acc + tile_sum(rhos[j][x + HALO, b] * y)
+            x0 = i * ROWS
+            for (x, h, b), d in smooth_rows(x0, ROWS, i * (ROWS // 2)):
+                y = eb[x0 + x + HALO, b, 8 + h * H : 8 + h * H + H, :] + d
+                put(db, None, 1, x0 + x, b, d, h)
+                ys[j][x0 + x, b, h * H : h * H + H, :] = y
+                acc = acc + tile_sum(rhos[j][x0 + x + HALO, b, h * H : h * H + H, :] * y)
             return acc
 
         return lax.fori_loop(0, NXL // ROWS, body, jnp.zeros((8, 128), F32))
@@ -432,21 +465,19 @@
         shift = HALO if j + 1 < ITERS else 0
 
         def rows(i, acc):
-            for x8 in range(ROWS):
-                x = i * ROWS + x8
-                insert(db, sd, 1, x)
-                new = []
-                for b in range(2):
-                    v = stencil(db, 1, x, b)
-                    rhos[j + 1][x + shift, b] = v
-                    acc = acc + tile_sum(v * ys[j][x, b])
-                    new.append(v)
-                    if j + 1 < ITERS:
-                        put_sides(ss.at[j + 1], x, b, v)
+            x0 = i * ROWS
+            for x in range(ROWS):
+                insert(db, sd, 1, x0 + x)
+            new = stencil_rows(db, 1, x0, ROWS)
+            for (x, h, b), v in new.items():
+                rhos[j + 1][x0 + x + shift, b, h * H : h * H + H, :] = v
+                acc = acc + tile_sum(v * ys[j][x0 + x, b, h * H : h * H + H, :])
                 if j + 1 < ITERS:
-                    e0 = split_mm(jnp.concatenate(new, axis=0), w0[...])
-                    put(e0b, cb0, HALO, x, 0, e0[:NY2])
-                    put(e0b, cb0, HALO, x, 1, e0[NY2:])
+                    put_sides(ss.at[j + 1], x0 + x, b, v, h)
+            if j + 1 < ITERS:
+                e0 = split_mm(jnp.concatenate(list(new.values()), axis=0), w0[...])
+                for n, (x, h, b) in enumerate(new):
+                    put(e0b, cb0, HALO, x0 + x, b, e0[n * H : n * H + H], h)
             return acc
 
         last = NXL // ROWS - 1
@@ -480,31 +511,20 @@
         rho, y = local(bars[(n + 1) // 2, here]), local(ybars[n // 2, here])
         v = nus[n] + 128.0 * jnp.sum((rho * y).reshape(4, 8, 128), axis=0)
         part = part + jnp.where(rows == n, jnp.sum(v, axis=0, keepdims=True), 0.0)
-    red1[0] = part
-
-    def sum_copies(buf, send_sems, recv_sems, devs):
-        return [
-            pltpu.make_async_remote_copy(
-                src_ref=buf.at[0], dst_ref=buf.at[i + 1], send_sem=send_sems.at[i],
-                recv_sem=recv_sems.at[i], device_id=dev, device_id_type=MESH,
+    total, copies = part, []
+    for n, devs in enumerate(phases):
+        red, base = reds[n], len(copies)
+        red[0] = total
+        for i, dev in enumerate(devs):
+            copy = pltpu.make_async_remote_copy(
+                src_ref=red.at[0], dst_ref=red.at[i + 1], send_sem=ss_sem.at[base + i],
+                recv_sem=rs_sem.at[base + i], device_id=dev, device_id_type=MESH,
             )
-            for i, dev in enumerate(devs)
-        ]
-
-    def sum_phase(copies, buf):
-        for copy in copies:
             copy.start()
-        for copy in copies:
+            copies.append(copy)
+        for copy in copies[base:]:
             copy.wait_recv()
-        total = buf[0]
-        for i in range(len(copies)):
-            total = total + buf[i + 1]
-        return total
-
-    copies1 = sum_copies(red1, s1_sem, r1_sem, [first_dev(*d) for d in first])
-    red2[0] = sum_phase(copies1, red1)
-    copies2 = sum_copies(red2, s2_sem, r2_sem, [second_dev(d) for d in second])
-    total = sum_phase(copies2, red2)
+        total = jnp.sum(red[...], axis=0)
     total = jnp.broadcast_to(jnp.sum(total, axis=1, keepdims=True), (8, 128))
     nu = [total[n : n + 1] for n in range(2 * ITERS)]
 
@@ -528,7 +548,6 @@
     to_columns(rbar)
     rcols = [tmat[pl.ds(b, NY2, stride=2), :] for b in range(2)]
 
-    outs = []
     for g in range(4):
         for x in range(8 * g, 8 * g + 8):
             for b in range(2):
@@ -538,41 +557,35 @@
                 ox = ox + c0 * ((1.0 - m) * v) + xcols[b][:, x : x + 1]
                 orr = a0 * v + a1 * rho1[x + HALO, b] + a2 * rho2[x + HALO, b] + c2 * rho3[x, b]
                 orr = orr + rcols[b][:, x : x + 1]
-                outx[x, pl.ds(b, NY2, stride=2), :] = ox
-                outr[x, pl.ds(b, NY2, stride=2), :] = orr
-        cells = pl.ds(8 * g, 8)
-        for i, (src, dst) in enumerate(((outx, x_ref), (outr, r_ref))):
-            copy = pltpu.make_async_copy(src.at[cells], dst.at[cells], out_sem.at[i, g])
-            copy.start()
-            outs.append(copy)
+                x_ref[x, pl.ds(b, NY2, stride=2), :] = ox
+                r_ref[x, pl.ds(b, NY2, stride=2), :] = orr
 
     for i in range(8):
         pl.when(exists(*SIDES[i]))(lambda i=i: block_copy(i).wait_send())
         for j in range(ITERS):
             pl.when(exists(*SIDES[i]))(lambda i=i, j=j: face(j, i).wait_send())
-    for copy in copies1 + copies2:
+    for copy in copies:
         copy.wait_send()
-    for copy in outs:
-        copy.wait()
 
 
 def shards(nx, ny, right_side, sea_mask, vertical_coupling):
     vmem = pltpu.VMEM
-    ng = nx // 4
-    n_first = 4 * ny - 1
-    out = jax.ShapeDtypeStruct(right_side.shape, F32)
+    sizes = {"x": nx // 8, "y": 4, "c": 2, "z": ny}
+    counts = [math.prod(sizes[axis] for axis in axes) for axes in PHASES]
+    counts = counts + [1] * (3 - len(counts))
+    out = pltpu.VMEM(right_side.shape, F32)
     return pl.pallas_call(
         functools.partial(kernel, nx, ny),
         out_shape=(out, out),
         in_specs=[
-            pl.BlockSpec(memory_space=pl.ANY),
-            pl.BlockSpec(memory_space=vmem),
-            pl.BlockSpec(memory_space=vmem),
+            pl.BlockSpec(memory_space=pltpu.HBM),
+            pl.BlockSpec(memory_space=pltpu.HBM),
+            pl.BlockSpec(memory_space=pltpu.HBM),
         ],
-        out_specs=(pl.BlockSpec(memory_space=pl.ANY), pl.BlockSpec(memory_space=pl.ANY)),
+        out_specs=(pl.BlockSpec(memory_space=vmem), pl.BlockSpec(memory_space=vmem)),
         scratch_shapes=[
-            vmem((NXL, 128, 128), F32),
-            vmem((NXL, 128, 128), F32),
+            vmem((NXL, 128), jnp.int32),
+            vmem((1, 127), F32),
             vmem((NXL, 128, 128), F32),
             vmem((NXL + 2 * HALO, 2, NY2, 128), F32),
             vmem((NXL + 2 * HALO, 2, NY2, 128), F32),
@@ -607,21 +620,17 @@
             vmem((ITERS + 1, 96, 256), F32),
             vmem((ITERS, 96, 256), F32),
             vmem((2 * ITERS, 8, 128), F32),
-            vmem((n_first + 1, 8, 128), F32),
-            vmem((ng, 8, 128), F32),
-            pltpu.SemaphoreType.DMA,
-            pltpu.SemaphoreType.DMA((2, 4)),
+            *[vmem((n, 8, 128), F32) for n in counts],
+            pltpu.SemaphoreType.DMA((3,)),
             pltpu.SemaphoreType.DMA((ITERS, 8)),
             pltpu.SemaphoreType.DMA((ITERS, 8)),
             pltpu.SemaphoreType.DMA((8,)),
             pltpu.SemaphoreType.DMA((8,)),
-            pltpu.SemaphoreType.DMA((n_first,)),
-            pltpu.SemaphoreType.DMA((n_first,)),
-            pltpu.SemaphoreType.DMA((ng - 1,)),
-            pltpu.SemaphoreType.DMA((ng - 1,)),
+            pltpu.SemaphoreType.DMA((sum(counts),)),
+            pltpu.SemaphoreType.DMA((sum(counts),)),
         ],
         compiler_params=pltpu.CompilerParams(
-            collective_id=0, has_side_effects=True, vmem_limit_bytes=60 * 1024 * 1024
+            collective_id=0, has_side_effects=True, vmem_limit_bytes=56 * 1024 * 1024
         ),
     )(right_side, sea_mask, vertical_coupling.reshape(1, -1))
 

time: 58.2 us -> 52.5 us (0.902)
  Pallas kernels: 52.6 us -> 49.1 us
  local copies, waits for them, and re-layouts: 4.61 us -> 2.64 us
    pallas_call x1, Pallas kernels: 52.6 us -> 49.1 us  [shards(): pl.pallas_call(functools.partial(kernel, nx, ny), out_shape=(out, out), i...]
    unnamed x4 -> x2, local copies, waits for them, and re-layouts: 4.61 us -> 2.64 us
where the time goes in v3:
time: 52.5 us; the launch traced here: 52.3 us
  Pallas kernels  49.1 us (94%)
  local copies, waits for them, and re-layouts  2.64 us (5%)
  between operations  0.64 us (1%)
    pallas_call x1, Pallas kernels, shards(): pl.pallas_call(functools.partial(kernel, nx, ny), out_shape=(out, out), i...  49.1 us
    unnamed x2, local copies, waits for them, and re-layouts  2.64 us

profile of v3, /device:TPU:0, one launch (start us, length us, event | category | flops | bytes accessed | tf_op | source)
XLA Modules:
  0.0 52.3 jit_solution(4628982655447296351)
XLA Ops:
  0.6 49.1 %shard_map.50 = (f32[32,128,128]{2,1,0:T(8,128)S(1)}, f32[32,128,128]{2,1,0:T(8,128)S(1)}) custom-call(f32[32,128,128]{2,1,0:T(8,128)} %rhs_ref.1, s32[32,128]{1,0:T(8,128)} %mask_hbm.1, f32[1,127]{1,0:T(1,128)} %bitcast.1), custom_call_target="tpu_custom_call" | custom-call | tf_op jit(solution)/shard_map/pallas_call | solution.py:577
  49.7 1.3 %copy.7 = f32[32,128,128]{2,1,0:T(8,128)} copy(f32[32,128,128]{2,1,0:T(8,128)S(1)} %get-tuple-element.2) | data formatting | bytes 4194304
  51.0 1.3 %copy.8 = f32[32,128,128]{2,1,0:T(8,128)} copy(f32[32,128,128]{2,1,0:T(8,128)S(1)} %get-tuple-element.3) | data formatting | bytes 4194304

commit v4 on v3

--- a/solution.py
+++ b/solution.py
@@ -18,7 +18,10 @@
 NXL, NY2, NZ = 32, 64, 128
 ROWS = 8
 HALO = 3
-H = 32
+EDGE = 4
+HALVES = ((0, 32), (32, 32))
+INNER = ((8, 24), (32, 24))
+OUTER = ((0, 8), (56, 8))
 PHASES = ("cz", "xy")
 SIDES = [(dx, dy) for dx in (-1, 0, 1) for dy in (-1, 0, 1) if (dx, dy) != (0, 0)]
 
@@ -95,7 +98,7 @@
     nx, ny, rhs_ref, mask_hbm, coup_hbm, x_ref, r_ref,
     mask_ref, coup_ref, inp, rho0, rho1, rho2, rho3, y0, y1, y2, e0b, eb, db, h1s, m3, q3,
     sr, ss, se0, se, sd, cb0, cb, sm, sq, w0, w1, kpad,
-    blk, nbr, tmat, mn, m2, bars, ybars, nus, red0, red1, red2,
+    blk, nbr, tmat, mn, m2, bars, ybars, nus, dots, cols, red0, red1, red2,
     in_sem, sx_sem, rx_sem, sb_sem, rb_sem, ss_sem, rs_sem,
 ):
     gx, gy = lax.axis_index("gx"), lax.axis_index("gy")
@@ -169,20 +172,19 @@
     to_columns(mask)
     expand(m3, 0, NXL, 2)
 
-    def put_sides(dst, x, b, v, h=None):
+    def put_sides(dst, x, b, v, y0=0):
         n = v.shape[0]
         for half, d, row in (
             ((0, 0, 0), (0, 2, 1), (1, 1, n - 1)) if b == 0 else ((0, 1, 0), (1, 0, n - 1), (1, 2, n - 2))
         ):
-            if h in (None, half):
+            if y0 == 0 if half == 0 else y0 + n == NY2:
                 dst[half, d, pl.ds(x, 1), :] = v[row : row + 1]
 
-    def put(dst, edge, shift, x, b, v, h=None):
-        y0, n = (8, NY2) if h is None else (8 + H * h, H)
-        dst[x + shift, b, y0 : y0 + n, :] = v
-        if edge is not None and h in (None, b):
-            row = v[0:1] if b == 0 else v[n - 1 : n]
-            edge[b, pl.ds(x + 8, 1), :] = row
+    def put(dst, edge, shift, x, b, v, y0=0):
+        n = v.shape[0]
+        dst[x + shift, b, 8 + y0 : 8 + y0 + n, :] = v
+        if edge is not None and (y0 == 0 if b == 0 else y0 + n == NY2):
+            edge[b, pl.ds(x + 8, 1), :] = v[0:1] if b == 0 else v[n - 1 : n]
 
     def tile_sum(v):
         return jnp.sum(v.reshape(-1, 8, 128), axis=0)
@@ -257,15 +259,18 @@
     send(0, along_x + corners + along_y)
     line_inverses(kpad[...], (w0, w1))
 
-    def line_pass0(i, carry):
-        for x8 in range(ROWS):
-            x = i * ROWS + x8
-            e0 = split_mm(rho0[x + HALO].reshape(128, 128), w0[...])
-            put(e0b, cb0, HALO, x, 0, e0[:NY2])
-            put(e0b, cb0, HALO, x, 1, e0[NY2:])
-        return carry
-
-    lax.fori_loop(0, NXL // ROWS, line_pass0, 0)
+    def line_pass(j):
+        def body(i, carry):
+            for x8 in range(ROWS):
+                x = i * ROWS + x8
+                e0 = split_mm(rhos[j][x + HALO].reshape(128, 128), w0[...])
+                put(e0b, cb0, HALO, x, 0, e0[:NY2])
+                put(e0b, cb0, HALO, x, 1, e0[NY2:])
+            return carry
+
+        lax.fori_loop(0, NXL // ROWS, body, 0)
+
+    line_pass(0)
 
     for i in range(8):
         dx, dy = SIDES[i]
@@ -350,28 +355,27 @@
         dst[x + shift, 1, 7:8, :] = src[0, pl.ds(x + 8, 1), :]
         dst[x + shift, 0, 72:73, :] = src[1, pl.ds(x + 8, 1), :]
 
-    def stencil_rows(src, shift, x0, count, less=None):
+    def stencil_rows(src, shift, x0, count, parts=HALVES, less=None):
         out = {}
-        for h in range(2):
-            y0 = 8 + H * h
+        for y0, n in parts:
             held = {}
 
             def centre(x, b):
                 if (x, b) not in held:
-                    held[x, b] = src[x0 + x + shift, b, y0 : y0 + H, :]
+                    held[x, b] = src[x0 + x + shift, b, 8 + y0 : 8 + y0 + n, :]
                 return held[x, b]
 
             for x in range(count):
-                minus = None if less is None else less(x, h)
+                minus = None if less is None else less(x, y0, n)
                 for b in range(2):
-                    at = y0 - 1 if b == 0 else y0 + 1
-                    beside = centre(x, 1 - b) + src[x0 + x + shift, 1 - b, at : at + H, :]
+                    at = 7 + y0 if b == 0 else 9 + y0
+                    beside = centre(x, 1 - b) + src[x0 + x + shift, 1 - b, at : at + n, :]
                     beside = beside + (centre(x - 1, b) + centre(x + 1, b))
                     if minus is not None:
                         beside = beside - minus
-                    q = q3[x0 + x + 2, b, H * h : H * h + H, :]
-                    m = m3[x0 + x + 2, b, H * h : H * h + H, :]
-                    out[x, h, b] = q * centre(x, b) + m * beside
+                    q = q3[x0 + x + 2, b, y0 : y0 + n, :]
+                    m = m3[x0 + x + 2, b, y0 : y0 + n, :]
+                    out[x, y0, b] = q * centre(x, b) + m * beside
         return out
 
     def strip_beside(v):
@@ -407,110 +411,136 @@
             rem.append(sq[s, 0] * near + sm[s, 0] * (cb[s] + far + strip_beside(near) - sd[s]))
         sd[...] = split_mm(jnp.concatenate(rem, axis=0), w0[...]).reshape(2, 48, 128)
 
-    def correct_pass():
+    def correct_block(first, count, parts):
+        x0 = 2 * first
+        t = stencil_rows(e0b, HALO, x0, 2 * count, parts)
+        keys = [(k, y0, n) for y0, n in parts for k in range(count)]
+        t1 = jnp.concatenate(
+            [
+                (t[2 * k, y0, 0] + t[2 * k, y0, 1]) + (t[2 * k + 1, y0, 0] + t[2 * k + 1, y0, 1])
+                for k, y0, n in keys
+            ],
+            axis=0,
+        )
+        e1 = split_mm(t1, w1[...])
+        h1 = 0.25 * t1 + 3.0 * e1
+        at = 0
+        for k, y0, n in keys:
+            part = e1[at : at + n]
+            h1s[first + k + 1, y0 : y0 + n, :] = h1[at : at + n]
+            at += n
+            for x in (2 * k, 2 * k + 1):
+                for b in range(2):
+                    m = m3[x0 + x + 2, b, y0 : y0 + n, :]
+                    e0 = e0b[x0 + x + HALO, b, 8 + y0 : 8 + y0 + n, :]
+                    put(eb, cb, HALO, x0 + x, b, e0 + m * part, y0)
+
+    def correct_inner():
         def body(i, carry):
-            x0 = i * 12 - 2
-            for x in range(12):
-                insert(e0b, se0.at[:, 0], HALO, x0 + x)
-            t = stencil_rows(e0b, HALO, x0, 12)
-            keys = [(k, h) for h in range(2) for k in range(6)]
-            t1 = jnp.concatenate(
-                [
-                    (t[2 * k, h, 0] + t[2 * k, h, 1]) + (t[2 * k + 1, h, 0] + t[2 * k + 1, h, 1])
-                    for k, h in keys
-                ],
-                axis=0,
-            )
-            e1 = split_mm(t1, w1[...])
-            h1 = 0.25 * t1 + 3.0 * e1
-            for n, (k, h) in enumerate(keys):
-                part = e1[n * H : n * H + H]
-                h1s[i * 6 + k, h * H : h * H + H, :] = h1[n * H : n * H + H]
-                for x in (2 * k, 2 * k + 1):
-                    for b in range(2):
-                        m = m3[x0 + x + 2, b, h * H : h * H + H, :]
-                        e0 = e0b[x0 + x + HALO, b, 8 + h * H : 8 + h * H + H, :]
-                        put(eb, cb, HALO, x0 + x, b, e0 + m * part, h)
+            correct_block(1 + 7 * i, 7, INNER)
             return carry
 
-        lax.fori_loop(0, 3, body, 0)
+        lax.fori_loop(0, 2, body, 0)
+
+    def correct_outer():
+        for x in range(-2, NXL + 2):
+            insert(e0b, se0.at[:, 0], HALO, x)
+        correct_block(-1, 2, HALVES)
+        correct_block(NXL // 2 - 1, 2, HALVES)
+        correct_block(1, 14, OUTER)
 
     def smooth_rows(x0, count, half0):
         for x in range(count):
             insert(eb, se.at[:, 0], HALO, x0 + x)
         rem = stencil_rows(
-            eb, HALO, x0, count,
-            lambda x, h: h1s[half0 + x // 2 + 1, h * H : h * H + H, :],
+            eb, HALO, x0, count, HALVES,
+            lambda x, y0, n: h1s[half0 + x // 2 + 1, y0 : y0 + n, :],
         )
         d = split_mm(jnp.concatenate(list(rem.values()), axis=0), w0[...])
-        return [(key, d[n * H : n * H + H]) for n, key in enumerate(rem)]
-
-    def smooth_pass(j):
+        return [(key, d[n * 32 : n * 32 + 32]) for n, key in enumerate(rem)]
+
+    def smooth_edges():
         for x0, half0 in ((-1, -1), (NXL, NXL // 2)):
-            for (x, h, b), d in smooth_rows(x0, 1, half0):
-                put(db, None, 1, x0 + x, b, d, h)
-
-        def body(i, acc):
-            x0 = i * ROWS
-            for (x, h, b), d in smooth_rows(x0, ROWS, i * (ROWS // 2)):
-                y = eb[x0 + x + HALO, b, 8 + h * H : 8 + h * H + H, :] + d
-                put(db, None, 1, x0 + x, b, d, h)
-                ys[j][x0 + x, b, h * H : h * H + H, :] = y
-                acc = acc + tile_sum(rhos[j][x0 + x + HALO, b, h * H : h * H + H, :] * y)
-            return acc
-
-        return lax.fori_loop(0, NXL // ROWS, body, jnp.zeros((8, 128), F32))
-
-    def next_pass(j):
+            for (x, y0, b), d in smooth_rows(x0, 1, half0):
+                put(db, None, 1, x0 + x, b, d, y0)
+
+    def smooth_part(j, i, acc):
+        x0 = i * ROWS
+        for (x, y0, b), d in smooth_rows(x0, ROWS, i * (ROWS // 2)):
+            y = eb[x0 + x + HALO, b, 8 + y0 : 40 + y0, :] + d
+            put(db, None, 1, x0 + x, b, d, y0)
+            ys[j][x0 + x, b, y0 : y0 + 32, :] = y
+            acc = acc + tile_sum(rhos[j][x0 + x + HALO, b, y0 : y0 + 32, :] * y)
+        return acc
+
+    def next_part(j, x0, count, acc):
         shift = HALO if j + 1 < ITERS else 0
-
-        def rows(i, acc):
-            x0 = i * ROWS
-            for x in range(ROWS):
-                insert(db, sd, 1, x0 + x)
-            new = stencil_rows(db, 1, x0, ROWS)
-            for (x, h, b), v in new.items():
-                rhos[j + 1][x0 + x + shift, b, h * H : h * H + H, :] = v
-                acc = acc + tile_sum(v * ys[j][x0 + x, b, h * H : h * H + H, :])
-                if j + 1 < ITERS:
-                    put_sides(ss.at[j + 1], x0 + x, b, v, h)
+        for x in range(count):
+            insert(db, sd, 1, x0 + x)
+        new = stencil_rows(db, 1, x0, count)
+        for (x, y0, b), v in new.items():
+            rhos[j + 1][x0 + x + shift, b, y0 : y0 + 32, :] = v
+            acc = acc + tile_sum(v * ys[j][x0 + x, b, y0 : y0 + 32, :])
             if j + 1 < ITERS:
-                e0 = split_mm(jnp.concatenate(list(new.values()), axis=0), w0[...])
-                for n, (x, h, b) in enumerate(new):
-                    put(e0b, cb0, HALO, x0 + x, b, e0[n * H : n * H + H], h)
-            return acc
-
+                put_sides(ss.at[j + 1], x0 + x, b, v, y0)
+        return acc
+
+    def smooth_and_next(j):
+        zero = jnp.zeros((8, 128), F32)
         last = NXL // ROWS - 1
-        acc = lax.fori_loop(0, 2, lambda i, a: rows(i * last, a), jnp.zeros((8, 128), F32))
+        smooth_edges()
+        acc = lax.fori_loop(0, 2, lambda i, a: smooth_part(j, i * last, a), zero)
+        acc_next = lax.fori_loop(0, 2, lambda i, a: next_part(j, i * (NXL - EDGE), EDGE, a), zero)
         if j + 1 < ITERS:
-            send(j + 1, along_x + corners)
-        acc = lax.fori_loop(1, last, rows, acc)
+            send(j + 1, along_x)
+        acc = lax.fori_loop(1, last, lambda i, a: smooth_part(j, i, a), acc)
+        nus[2 * j] = acc
+        acc_next = lax.fori_loop(
+            0, 3, lambda i, a: next_part(j, EDGE + i * ROWS, ROWS, a), acc_next
+        )
         if j + 1 < ITERS:
-            send(j + 1, along_y)
-        return acc
+            send(j + 1, corners + along_y)
+        nus[2 * j + 1] = acc_next
+
+    dot_rows = lax.broadcasted_iota(jnp.int32, (8, 128), 0)
+    here = pl.ds(32, NXL)
+
+    def dot_row(n, v):
+        return jnp.where(dot_rows == n, jnp.sum(v, axis=0, keepdims=True), 0.0)
+
+    def mean_results():
+        bar = [local(bars[n, here]) for n in range(ITERS + 1)]
+        ybar = [local(ybars[n, here]) for n in range(ITERS)]
+        part = dot_row(0, nu0)
+        for n in range(2 * ITERS):
+            v = 128.0 * tile_sum(bar[(n + 1) // 2] * ybar[n // 2])
+            part = part + dot_row(n, v + nus[n] if n < 4 else v)
+        dots[...] = part
+        for n, v in enumerate(ybar + bar[1:]):
+            to_columns(v)
+            for b in range(2):
+                cols[n, b] = tmat[pl.ds(b, NY2, stride=2), :]
 
     for j in range(ITERS):
+        if j > 0:
+            line_pass(j)
+        correct_inner()
+        if j == 1:
+            mean_step(0)
+            mean_step(1)
+        if j == 2:
+            mean_step(2)
+            mean_results()
         receive(j)
         halo_lines(j)
         strip_correct()
-        correct_pass()
+        correct_outer()
         strip_smooth()
-        acc = smooth_pass(j)
-        nus[2 * j] = acc + nu0 if j == 0 else acc
-        nus[2 * j + 1] = next_pass(j)
-        if j == 0:
-            mean_step(0)
-            mean_step(1)
-        if j == 1:
-            mean_step(2)
-
-    rows = lax.broadcasted_iota(jnp.int32, (8, 128), 0)
-    part = jnp.zeros((8, 128), F32)
-    here = pl.ds(32, NXL)
-    for n in range(2 * ITERS):
-        rho, y = local(bars[(n + 1) // 2, here]), local(ybars[n // 2, here])
-        v = nus[n] + 128.0 * jnp.sum((rho * y).reshape(4, 8, 128), axis=0)
-        part = part + jnp.where(rows == n, jnp.sum(v, axis=0, keepdims=True), 0.0)
+        smooth_and_next(j)
+
+    part = dots[...]
+    for n in (4, 5):
+        part = part + dot_row(n, nus[n])
     total, copies = part, []
     for n, devs in enumerate(phases):
         red, base = reds[n], len(copies)
@@ -541,12 +571,8 @@
     c0 = nu[0] / h00 - l10 * c1 - l20 * c2
     a0, a1, a2 = 1.0 - c0, c0 - c1, c1 - c2
 
-    xbar = c0 * local(ybars[0, here]) + c1 * local(ybars[1, here]) + c2 * local(ybars[2, here])
-    rbar = a1 * local(bars[1, here]) + a2 * local(bars[2, here]) + c2 * local(bars[3, here])
-    to_columns(xbar)
-    xcols = [tmat[pl.ds(b, NY2, stride=2), :] for b in range(2)]
-    to_columns(rbar)
-    rcols = [tmat[pl.ds(b, NY2, stride=2), :] for b in range(2)]
+    xcols = [c0 * cols[0, b] + c1 * cols[1, b] + c2 * cols[2, b] for b in range(2)]
+    rcols = [a1 * cols[3, b] + a2 * cols[4, b] + c2 * cols[5, b] for b in range(2)]
 
     for g in range(4):
         for x in range(8 * g, 8 * g + 8):
@@ -620,6 +646,8 @@
             vmem((ITERS + 1, 96, 256), F32),
             vmem((ITERS, 96, 256), F32),
             vmem((2 * ITERS, 8, 128), F32),
+            vmem((8, 128), F32),
+            vmem((2 * ITERS, 2, NY2, 128), F32),
             *[vmem((n, 8, 128), F32) for n in counts],
             pltpu.SemaphoreType.DMA((3,)),
             pltpu.SemaphoreType.DMA((ITERS, 8)),

time: 52.5 us -> 47.6 us (0.907)
  Pallas kernels: 49.1 us -> 44.2 us
    pallas_call x1, Pallas kernels: 49.1 us -> 44.2 us  [shards(): pl.pallas_call(functools.partial(kernel, nx, ny), out_shape=(out, out), i...]
where the time goes in v4:
time: 47.6 us; the launch traced here: 47.5 us
  Pallas kernels  44.2 us (93%)
  local copies, waits for them, and re-layouts  2.64 us (6%)
  between operations  0.64 us (1%)
    pallas_call x1, Pallas kernels, shards(): pl.pallas_call(functools.partial(kernel, nx, ny), out_shape=(out, out), i...  44.2 us
    unnamed x2, local copies, waits for them, and re-layouts  2.64 us

profile of v4, /device:TPU:0, one launch (start us, length us, event | category | flops | bytes accessed | tf_op | source)
XLA Modules:
  0.0 47.5 jit_solution(12360466604657683177)
XLA Ops:
  0.6 44.2 %shard_map.50 = (f32[32,128,128]{2,1,0:T(8,128)S(1)}, f32[32,128,128]{2,1,0:T(8,128)S(1)}) custom-call(f32[32,128,128]{2,1,0:T(8,128)} %rhs_ref.1, s32[32,128]{1,0:T(8,128)} %mask_hbm.1, f32[1,127]{1,0:T(1,128)} %bitcast.1), custom_call_target="tpu_custom_call" | custom-call | tf_op jit(solution)/shard_map/pallas_call | solution.py:603
  44.8 1.3 %copy.7 = f32[32,128,128]{2,1,0:T(8,128)} copy(f32[32,128,128]{2,1,0:T(8,128)S(1)} %get-tuple-element.2) | data formatting | bytes 4194304
  46.1 1.3 %copy.8 = f32[32,128,128]{2,1,0:T(8,128)} copy(f32[32,128,128]{2,1,0:T(8,128)S(1)} %get-tuple-element.3) | data formatting | bytes 4194304

commit v5 on v4

--- a/solution.py
+++ b/solution.py
@@ -249,6 +249,12 @@
     def send(j, which):
         for i in which:
             pl.when(exists(*SIDES[i]))(lambda i=i: face(j, i).start())
+
+    def sent(j):
+        for i in range(8):
+            pl.when(exists(*SIDES[i]))(lambda i=i: face(j, i).wait_send())
+            if j == 0:
+                pl.when(exists(*SIDES[i]))(lambda i=i: block_copy(i).wait_send())
 
     def receive(j):
         for i, (dx, dy) in enumerate(SIDES):
@@ -449,28 +455,37 @@
         correct_block(NXL // 2 - 1, 2, HALVES)
         correct_block(1, 14, OUTER)
 
-    def smooth_rows(x0, count, half0):
+    def smooth_rows(x0, count, half):
         for x in range(count):
             insert(eb, se.at[:, 0], HALO, x0 + x)
         rem = stencil_rows(
             eb, HALO, x0, count, HALVES,
-            lambda x, y0, n: h1s[half0 + x // 2 + 1, y0 : y0 + n, :],
+            lambda x, y0, n: h1s[half(x) + 1, y0 : y0 + n, :],
         )
         d = split_mm(jnp.concatenate(list(rem.values()), axis=0), w0[...])
         return [(key, d[n * 32 : n * 32 + 32]) for n, key in enumerate(rem)]
 
-    def smooth_edges():
-        for x0, half0 in ((-1, -1), (NXL, NXL // 2)):
-            for (x, y0, b), d in smooth_rows(x0, 1, half0):
-                put(db, None, 1, x0 + x, b, d, y0)
+    def smooth_put(j, x, y0, b, d, acc):
+        y = eb[x + HALO, b, 8 + y0 : 40 + y0, :] + d
+        put(db, None, 1, x, b, d, y0)
+        ys[j][x, b, y0 : y0 + 32, :] = y
+        return acc + tile_sum(rhos[j][x + HALO, b, y0 : y0 + 32, :] * y)
+
+    def smooth_edges(j, acc):
+        for x0 in (-1, NXL - EDGE):
+            for (x, y0, b), d in smooth_rows(x0, EDGE + 1, lambda x: (x0 + x) // 2):
+                if 0 <= x0 + x < NXL:
+                    acc = smooth_put(j, x0 + x, y0, b, d, acc)
+                else:
+                    put(db, None, 1, x0 + x, b, d, y0)
+        return acc
 
     def smooth_part(j, i, acc):
-        x0 = i * ROWS
-        for (x, y0, b), d in smooth_rows(x0, ROWS, i * (ROWS // 2)):
-            y = eb[x0 + x + HALO, b, 8 + y0 : 40 + y0, :] + d
-            put(db, None, 1, x0 + x, b, d, y0)
-            ys[j][x0 + x, b, y0 : y0 + 32, :] = y
-            acc = acc + tile_sum(rhos[j][x0 + x + HALO, b, y0 : y0 + 32, :] * y)
+        x0 = EDGE + i * ROWS
+        for (x, y0, b), d in smooth_rows(
+            x0, ROWS, lambda x: EDGE // 2 + i * (ROWS // 2) + x // 2
+        ):
+            acc = smooth_put(j, x0 + x, y0, b, d, acc)
         return acc
 
     def next_part(j, x0, count, acc):
@@ -487,16 +502,15 @@
 
     def smooth_and_next(j):
         zero = jnp.zeros((8, 128), F32)
-        last = NXL // ROWS - 1
-        smooth_edges()
-        acc = lax.fori_loop(0, 2, lambda i, a: smooth_part(j, i * last, a), zero)
-        acc_next = lax.fori_loop(0, 2, lambda i, a: next_part(j, i * (NXL - EDGE), EDGE, a), zero)
+        acc = smooth_edges(j, zero)
+        acc_next = next_part(j, 0, HALO, zero)
+        acc_next = next_part(j, NXL - HALO, HALO, acc_next)
         if j + 1 < ITERS:
             send(j + 1, along_x)
-        acc = lax.fori_loop(1, last, lambda i, a: smooth_part(j, i, a), acc)
-        nus[2 * j] = acc
+        nus[2 * j] = lax.fori_loop(0, 3, lambda i, a: smooth_part(j, i, a), acc)
+        inner = (NXL - 2 * HALO) // 2
         acc_next = lax.fori_loop(
-            0, 3, lambda i, a: next_part(j, EDGE + i * ROWS, ROWS, a), acc_next
+            0, 2, lambda i, a: next_part(j, HALO + i * inner, inner, a), acc_next
         )
         if j + 1 < ITERS:
             send(j + 1, corners + along_y)
@@ -524,6 +538,7 @@
     for j in range(ITERS):
         if j > 0:
             line_pass(j)
+            sent(j - 1)
         correct_inner()
         if j == 1:
             mean_step(0)
@@ -548,12 +563,16 @@
         for i, dev in enumerate(devs):
             copy = pltpu.make_async_remote_copy(
                 src_ref=red.at[0], dst_ref=red.at[i + 1], send_sem=ss_sem.at[base + i],
-                recv_sem=rs_sem.at[base + i], device_id=dev, device_id_type=MESH,
+                recv_sem=rs_sem.at[n], device_id=dev, device_id_type=MESH,
             )
             copy.start()
             copies.append(copy)
-        for copy in copies[base:]:
-            copy.wait_recv()
+        if n == 1:
+            sent(ITERS - 1)
+            for copy in copies[:base]:
+                copy.wait_send()
+        rest = red.at[pl.ds(1, len(devs))]
+        pltpu.make_async_copy(rest, rest, rs_sem.at[n]).wait()
         total = jnp.sum(red[...], axis=0)
     total = jnp.broadcast_to(jnp.sum(total, axis=1, keepdims=True), (8, 128))
     nu = [total[n : n + 1] for n in range(2 * ITERS)]
@@ -586,11 +605,7 @@
                 x_ref[x, pl.ds(b, NY2, stride=2), :] = ox
                 r_ref[x, pl.ds(b, NY2, stride=2), :] = orr
 
-    for i in range(8):
-        pl.when(exists(*SIDES[i]))(lambda i=i: block_copy(i).wait_send())
-        for j in range(ITERS):
-            pl.when(exists(*SIDES[i]))(lambda i=i, j=j: face(j, i).wait_send())
-    for copy in copies:
+    for copy in copies[len(phases[0]):]:
         copy.wait_send()
 
 
@@ -655,7 +670,7 @@
             pltpu.SemaphoreType.DMA((8,)),
             pltpu.SemaphoreType.DMA((8,)),
             pltpu.SemaphoreType.DMA((sum(counts),)),
-            pltpu.SemaphoreType.DMA((sum(counts),)),
+            pltpu.SemaphoreType.DMA((2,)),
         ],
         compiler_params=pltpu.CompilerParams(
             collective_id=0, has_side_effects=True, vmem_limit_bytes=56 * 1024 * 1024

time: 47.6 us -> 46.1 us (0.968)
  Pallas kernels: 44.2 us -> 42.7 us
    pallas_call x1, Pallas kernels: 44.2 us -> 42.7 us  [shards(): pl.pallas_call(functools.partial(kernel, nx, ny), out_shape=(out, out), i...]
where the time goes in v5:
time: 46.1 us; the launch traced here: 45.9 us
  Pallas kernels  42.7 us (93%)
  local copies, waits for them, and re-layouts  2.64 us (6%)
  between operations  0.64 us (1%)
    pallas_call x1, Pallas kernels, shards(): pl.pallas_call(functools.partial(kernel, nx, ny), out_shape=(out, out), i...  42.7 us
    unnamed x2, local copies, waits for them, and re-layouts  2.64 us

profile of v5, /device:TPU:0, one launch (start us, length us, event | category | flops | bytes accessed | tf_op | source)
XLA Modules:
  0.0 45.9 jit_solution(16548935471561966184)
XLA Ops:
  0.6 42.7 %shard_map.50 = (f32[32,128,128]{2,1,0:T(8,128)S(1)}, f32[32,128,128]{2,1,0:T(8,128)S(1)}) custom-call(f32[32,128,128]{2,1,0:T(8,128)} %rhs_ref.1, s32[32,128]{1,0:T(8,128)} %mask_hbm.1, f32[1,127]{1,0:T(1,128)} %bitcast.1), custom_call_target="tpu_custom_call" | custom-call | tf_op jit(solution)/shard_map/pallas_call | solution.py:618
  43.3 1.3 %copy.7 = f32[32,128,128]{2,1,0:T(8,128)} copy(f32[32,128,128]{2,1,0:T(8,128)S(1)} %get-tuple-element.2) | data formatting | bytes 4194304
  44.6 1.3 %copy.8 = f32[32,128,128]{2,1,0:T(8,128)} copy(f32[32,128,128]{2,1,0:T(8,128)S(1)} %get-tuple-element.3) | data formatting | bytes 4194304

commit v6 on v5

--- a/solution.py
+++ b/solution.py
@@ -19,6 +19,7 @@
 ROWS = 8
 HALO = 3
 EDGE = 4
+MID = 12
 HALVES = ((0, 32), (32, 32))
 INNER = ((8, 24), (32, 24))
 OUTER = ((0, 8), (56, 8))
@@ -267,14 +268,14 @@
 
     def line_pass(j):
         def body(i, carry):
-            for x8 in range(ROWS):
-                x = i * ROWS + x8
+            for x8 in range(2 * ROWS):
+                x = i * 2 * ROWS + x8
                 e0 = split_mm(rhos[j][x + HALO].reshape(128, 128), w0[...])
                 put(e0b, cb0, HALO, x, 0, e0[:NY2])
                 put(e0b, cb0, HALO, x, 1, e0[NY2:])
             return carry
 
-        lax.fori_loop(0, NXL // ROWS, body, 0)
+        lax.fori_loop(0, NXL // (2 * ROWS), body, 0)
 
     line_pass(0)
 
@@ -442,11 +443,7 @@
                     put(eb, cb, HALO, x0 + x, b, e0 + m * part, y0)
 
     def correct_inner():
-        def body(i, carry):
-            correct_block(1 + 7 * i, 7, INNER)
-            return carry
-
-        lax.fori_loop(0, 2, body, 0)
+        correct_block(1, NXL // 2 - 2, INNER)
 
     def correct_outer():
         for x in range(-2, NXL + 2):
@@ -481,9 +478,9 @@
         return acc
 
     def smooth_part(j, i, acc):
-        x0 = EDGE + i * ROWS
+        x0 = EDGE + i * MID
         for (x, y0, b), d in smooth_rows(
-            x0, ROWS, lambda x: EDGE // 2 + i * (ROWS // 2) + x // 2
+            x0, MID, lambda x: EDGE // 2 + i * (MID // 2) + x // 2
         ):
             acc = smooth_put(j, x0 + x, y0, b, d, acc)
         return acc
@@ -507,7 +504,7 @@
         acc_next = next_part(j, NXL - HALO, HALO, acc_next)
         if j + 1 < ITERS:
             send(j + 1, along_x)
-        nus[2 * j] = lax.fori_loop(0, 3, lambda i, a: smooth_part(j, i, a), acc)
+        nus[2 * j] = lax.fori_loop(0, (NXL - 2 * EDGE) // MID, lambda i, a: smooth_part(j, i, a), acc)
         inner = (NXL - 2 * HALO) // 2
         acc_next = lax.fori_loop(
             0, 2, lambda i, a: next_part(j, HALO + i * inner, inner, a), acc_next

time: 46.1 us -> 46 us (level)
  no operation moved by 1% of the time
where the time goes in v6:
time: 46 us; the launch traced here: 45.9 us
  Pallas kernels  42.6 us (93%)
  local copies, waits for them, and re-layouts  2.64 us (6%)
  between operations  0.64 us (1%)
    pallas_call x1, Pallas kernels, shards(): pl.pallas_call(functools.partial(kernel, nx, ny), out_shape=(out, out), i...  42.6 us
    unnamed x2, local copies, waits for them, and re-layouts  2.64 us

profile of v6, /device:TPU:0, one launch (start us, length us, event | category | flops | bytes accessed | tf_op | source)
XLA Modules:
  0.0 45.9 jit_solution(7177456800268021100)
XLA Ops:
  0.6 42.6 %shard_map.50 = (f32[32,128,128]{2,1,0:T(8,128)S(1)}, f32[32,128,128]{2,1,0:T(8,128)S(1)}) custom-call(f32[32,128,128]{2,1,0:T(8,128)} %rhs_ref.1, s32[32,128]{1,0:T(8,128)} %mask_hbm.1, f32[1,127]{1,0:T(1,128)} %bitcast.1), custom_call_target="tpu_custom_call" | custom-call | tf_op jit(solution)/shard_map/pallas_call | solution.py:615
  43.2 1.3 %copy.7 = f32[32,128,128]{2,1,0:T(8,128)} copy(f32[32,128,128]{2,1,0:T(8,128)S(1)} %get-tuple-element.2) | data formatting | bytes 4194304
  44.5 1.3 %copy.8 = f32[32,128,128]{2,1,0:T(8,128)} copy(f32[32,128,128]{2,1,0:T(8,128)S(1)} %get-tuple-element.3) | data formatting | bytes 4194304
